TPU v7x, 32 devices: a whole 2x2x4 slice. The times are simulated.
32 devices in a mesh: seq: 16 (over z, y, x), dp: 2 (over core).
Axes of the slice: x: 2, y: 2, z: 4, core: 2. Of those that a mesh axis runs over, the one named last changes fastest.
Arguments:
- query_proj: bfloat16 [10240, 1024], P(('dp', 'seq')), parts along dimension 0, may hold values from -8 to 8
- key_proj: bfloat16 [10240, 1024], P(('dp', 'seq')), parts along dimension 0, may hold values from -8 to 8
- value_proj: bfloat16 [10240, 1024], P(('dp', 'seq')), parts along dimension 0, may hold values from -6 to 6
- residual_in: bfloat16 [10240, 1024], P(('dp', 'seq')), parts along dimension 0, may hold values from -6 to 6
- utter_lengths: int32 [32], P('dp'), parts along dimension 0, may hold values from 1 to 640, 5120 in all
- depth_kernel: float32 [31, 1024], replicated, may hold values from -1 to 1
- norm_gain: float32 [1024], replicated, may hold values from 0.5 to 1.5
- norm_shift: float32 [1024], replicated, may hold values from -3 to 3
Outputs:
- block_out: bfloat16 [10240, 1024], P(('dp', 'seq')), parts along dimension 0
There are 2 independent parts, one for each index of `dp`. A program takes and returns all parts, laid end to end along the dimension named above; an argument that names none is the same for every part. Nothing has to cross between parts.
Inputs may be any that keep to these rules, and one draw needn't show every extreme that they name: `utter_lengths`: the lengths sum to 5120; the largest is exactly 640.
All inputs are finite; a program needn't handle non-finite values.
Results may differ from a plain program's by a relative error of at most 0.005.
Values may be sent and summed in bfloat16 or wider, within the bound.
No kernel may reach another device: no remote copies, remote signals or barrier semaphores. Data moves between devices by JAX's collectives and lax.ppermute only.
A program may use at most 64 MiB of HBM per device.

v0:
```python
import jax
import jax.numpy as jnp
from jax import lax
from jax.sharding import PartitionSpec as P

HD = 64


def passed_along(array, axis, by):
    peers = lax.axis_size(axis)
    pairs = [(i, i + by) for i in range(peers) if 0 <= i + by < peers]
    return lax.ppermute(array, axis, pairs)


def extended(array, sides, width):
    for axis, dim in sides:
        peers, length = (lax.axis_size(axis), array.shape[dim])
        up = [(i, (i + 1) % peers) for i in range(peers - 1)]
        down = [(j, i) for i, j in up]
        last = lax.slice_in_dim(array, length - width, length, axis=dim)
        initial = lax.slice_in_dim(array, 0, width, axis=dim)
        before = lax.ppermute(last, axis, up)
        after = lax.ppermute(initial, axis, down)
        array = jnp.concatenate([before, array, after], axis=dim)
    return array


def utterance_ids(positions, utt_ends, frames_all):
    counted = jnp.sum((utt_ends[None, :] <= positions[:, None]).astype(jnp.int32), axis=1)
    inside = (positions >= 0) & (positions < frames_all)
    return jnp.where(inside, counted, -1)


def attend(query_rows, query_pos, key_rows, value_rows, key_pos, utt_ends, frames_all):
    query_utt = utterance_ids(query_pos, utt_ends, frames_all)
    key_utt = utterance_ids(key_pos, utt_ends, frames_all)
    same_utt = (query_utt[:, None] == key_utt[None, :])[None]
    score_scale = HD ** (-0.5)
    group_width = 2 * HD
    pieces = []
    for first_col in range(0, query_rows.shape[1], group_width):
        query_group = query_rows[:, first_col : first_col + group_width].reshape(-1, 2, HD)
        key_group = key_rows[:, first_col : first_col + group_width].reshape(-1, 2, HD)
        value_group = value_rows[:, first_col : first_col + group_width].reshape(-1, 2, HD)
        scores = (
            jnp.einsum("qhd,khd->hqk", query_group, key_group, preferred_element_type=jnp.float32)
            * score_scale
        )
        scores = jnp.where(same_utt, scores, jnp.float32(-1e30))
        row_max = jnp.max(scores, axis=-1, keepdims=True)
        probs = jnp.where(same_utt, jnp.exp(scores - row_max), jnp.float32(0.0))
        denom = jnp.sum(probs, axis=-1)
        weights = probs.astype(jnp.bfloat16)
        context = (
            jnp.einsum("hqk,khd->qhd", weights, value_group, preferred_element_type=jnp.float32)
            / denom.T[:, :, None]
        )
        pieces.append(context.reshape(context.shape[0], group_width))
    return jnp.concatenate(pieces, axis=1)


def local(
    query_proj,
    key_proj,
    value_proj,
    residual_in,
    utter_lengths,
    depth_kernel,
    norm_gain,
    norm_shift,
):
    n_rows = query_proj.shape[0]
    frames_all = n_rows * lax.axis_size("seq")
    dev_index = lax.axis_index("seq")
    utt_ends = jnp.cumsum(utter_lengths)
    half_width = depth_kernel.shape[0] // 2
    own_pair = (key_proj, value_proj)
    received = {}
    for shift_by in (2, 1, -1, -2):
        received[shift_by] = passed_along((own_pair[0], own_pair[1]), "seq", shift_by)
    ordered = [received[2], received[1], own_pair, received[-1], received[-2]]
    key_rows = jnp.concatenate([pair[0] for pair in ordered], axis=0)
    value_rows = jnp.concatenate([pair[1] for pair in ordered], axis=0)
    first_key = dev_index * n_rows - 2 * n_rows
    key_pos = first_key + jnp.arange(key_rows.shape[0], dtype=jnp.int32)
    query_pos = dev_index * n_rows + jnp.arange(n_rows, dtype=jnp.int32)
    context = attend(query_proj, query_pos, key_rows, value_rows, key_pos, utt_ends, frames_all)
    mixed = (residual_in.astype(jnp.float32) + context).astype(jnp.bfloat16)
    mixed_padded = extended(mixed, (("seq", 0),), half_width)
    padded_pos = (
        dev_index * n_rows - half_width + jnp.arange(n_rows + 2 * half_width, dtype=jnp.int32)
    )
    padded_utt = utterance_ids(padded_pos, utt_ends, frames_all)
    own_utt = padded_utt[half_width : half_width + n_rows]
    conv_sum = jnp.zeros(mixed.shape, jnp.float32)
    for tap in range(depth_kernel.shape[0]):
        same_utt = padded_utt[tap : tap + n_rows] == own_utt
        term = mixed_padded[tap : tap + n_rows].astype(jnp.float32) * depth_kernel[tap][None, :]
        conv_sum = conv_sum + jnp.where(same_utt[:, None], term, jnp.float32(0.0))
    mean_val = jnp.mean(conv_sum, axis=1, keepdims=True)
    centred = conv_sum - mean_val
    var_val = jnp.mean(centred * centred, axis=1, keepdims=True)
    normed = centred / jnp.sqrt(var_val + 1e-05) * norm_gain[None, :] + norm_shift[None, :]
    return (mixed.astype(jnp.float32) + normed * jax.nn.sigmoid(normed)).astype(jnp.bfloat16)


def solution(mesh):
    return jax.shard_map(
        local,
        mesh=mesh,
        in_specs=(
            P(("dp", "seq"), None),
            P(("dp", "seq"), None),
            P(("dp", "seq"), None),
            P(("dp", "seq"), None),
            P("dp"),
            P(),
            P(),
            P(),
        ),
        out_specs=P(("dp", "seq"), None),
        check_vma=False,
    )
```

profile of v0, /device:TPU:16, one launch (start us, length us, event | category | flops | bytes accessed | tf_op | source)
XLA Modules:
  0.0 215.4 jit_solution(10779614602461703399)
XLA Ops:
  0.0 3.4 %collective-permute-start = (bf16[320,1024]{1,0:T(8,128)(2,1)}, bf16[320,1024]{1,0:T(8,128)(2,1)}, u32[]{:S(2)}, u32[]{:S(2)}) collective-permute-start(bf16[320,1024]{1,0:T(8,128)(2,1)} %param.10), channel_id=1, source_target_pairs={{0,4},{2,6},{4,8},{6,10},{8,12},{10,14},{12,16},{14,18},{16,20},{1... | collective-permute-start | bytes 1966088 | tf_op jit(solution)/shard_map/ppermute | solution.py:12
  3.4 3.4 %collective-permute-start.1 = (bf16[320,1024]{1,0:T(8,128)(2,1)}, bf16[320,1024]{1,0:T(8,128)(2,1)S(1)}, u32[]{:S(2)}, u32[]{:S(2)}) collective-permute-start(bf16[320,1024]{1,0:T(8,128)(2,1)} %param.10), channel_id=1, source_target_pairs={{0,2},{2,4},{4,6},{6,8},{8,10},{10,12},{12,14},{14,16},{16,18},{18... | collective-permute-start | bytes 1966088 | tf_op jit(solution)/shard_map/ppermute | solution.py:12
  6.8 4.2 %collective-permute-start.2 = (bf16[320,1024]{1,0:T(8,128)(2,1)}, bf16[320,1024]{1,0:T(8,128)(2,1)S(1)}, u32[]{:S(2)}, u32[]{:S(2)}) collective-permute-start(bf16[320,1024]{1,0:T(8,128)(2,1)} %param.10), channel_id=1, source_target_pairs={{2,0},{4,2},{6,4},{8,6},{10,8},{12,10},{14,12},{16,14},{18,16},{20... | collective-permute-start | bytes 1966088 | tf_op jit(solution)/shard_map/ppermute | solution.py:12
  13.5 3.4 %collective-permute-start.4 = (bf16[320,1024]{1,0:T(8,128)(2,1)}, bf16[320,1024]{1,0:T(8,128)(2,1)S(1)}, u32[]{:S(2)}, u32[]{:S(2)}) collective-permute-start(bf16[320,1024]{1,0:T(8,128)(2,1)} %param.9), channel_id=1, source_target_pairs={{0,4},{2,6},{4,8},{6,10},{8,12},{10,14},{12,16},{14,18},{16,20},{1... | collective-permute-start | bytes 1966088 | tf_op jit(solution)/shard_map/ppermute | solution.py:12
  38.9 11.4 %collective-permute-start.5 = (bf16[320,1024]{1,0:T(8,128)(2,1)S(1)}, bf16[320,1024]{1,0:T(8,128)(2,1)}, u32[]{:S(2)}, u32[]{:S(2)}) collective-permute-start(bf16[320,1024]{1,0:T(8,128)(2,1)S(1)} %copy-done.4), channel_id=1, source_target_pairs={{0,2},{2,4},{4,6},{6,8},{8,10},{10,12},{12,14},{14,16},{16,18},{18... | collective-permute-start | bytes 1966088 | tf_op jit(solution)/shard_map/ppermute | solution.py:12
  51.5 3.7 %collective-permute-start.6 = (bf16[320,1024]{1,0:T(8,128)(2,1)S(1)}, bf16[320,1024]{1,0:T(8,128)(2,1)}, u32[]{:S(2)}, u32[]{:S(2)}) collective-permute-start(bf16[320,1024]{1,0:T(8,128)(2,1)S(1)} %copy-done.4), channel_id=1, source_target_pairs={{2,0},{4,2},{6,4},{8,6},{10,8},{12,10},{14,12},{16,14},{18,16},{20... | collective-permute-start | bytes 1966088 | tf_op jit(solution)/shard_map/ppermute | solution.py:12
  58.3 17.4 %collective-permute-done.3 = bf16[320,1024]{1,0:T(8,128)(2,1)S(1)} collective-permute-done((bf16[320,1024]{1,0:T(8,128)(2,1)}, bf16[320,1024]{1,0:T(8,128)(2,1)S(1)}, u32[]{:S(2)}, u32[]{:S(2)}) %collective-permute-start.3) | collective-permute-done | bytes 655392 | tf_op jit(solution)/shard_map/ppermute | solution.py:12
  80.7 9.1 %collective-permute-done.7 = bf16[320,1024]{1,0:T(8,128)(2,1)} collective-permute-done((bf16[320,1024]{1,0:T(8,128)(2,1)S(1)}, bf16[320,1024]{1,0:T(8,128)(2,1)}, u32[]{:S(2)}, u32[]{:S(2)}) %collective-permute-start.7) | collective-permute-done | bytes 655392 | tf_op jit(solution)/shard_map/ppermute | solution.py:12
  104.3 3.6 %fusion.238 = f32[2,320]{1,0:T(2,128)S(1)} fusion(pred[320,1600]{1,0:T(8,128)(4,1)} %broadcast_compare_fusion, bf16[1600,2,64]{0,2,1:T(8,128)(2,1)} %bitcast.244, bf16[320,2,64]{0,2,1:T(8,128)(2,1)} %bitcast.276), kind=kOutput, calls=%fused_computation.308 | convolution fusion | flops 136193600 | bytes 1006080 | tf_op jit(solution)/shard_map/sub | solution.py:51
  108.0 4.4 %fusion.82 = f32[320,2,64]{0,2,1:T(8,128)} fusion(bf16[1600,2,64]{0,2,1:T(8,128)(2,1)} %bitcast.234, pred[320,1600]{1,0:T(8,128)(4,1)} %broadcast_compare_fusion, bf16[1600,2,64]{0,2,1:T(8,128)(2,1)} %bitcast.245, bf16[320,2,64]{0,2,1:T(8,128)(2,1)} %bitcast.277, f32[320,2]{0,1:T(2,128)S(1)} %bitcast.314), kind=kOutput, calls=%fused_computation.124 | convolution fusion | flops 267307200 | bytes 1579520 | tf_op jit(solution)/shard_map/hqk,khd->qhd/dot_general | solution.py:55
  117.3 4.4 %fusion.239 = f32[2,320]{1,0:T(2,128)} fusion(pred[320,1600]{1,0:T(8,128)(4,1)} %broadcast_compare_fusion, bf16[1600,2,64]{0,2,1:T(8,128)(2,1)} %bitcast.246, bf16[320,2,64]{0,2,1:T(8,128)(2,1)} %bitcast.274), kind=kOutput, calls=%fused_computation.309 | convolution fusion | flops 136193600 | bytes 1006080 | tf_op jit(solution)/shard_map/sub | solution.py:51
  121.7 4.3 %fusion.88 = f32[320,2,64]{0,2,1:T(8,128)} fusion(bf16[1600,2,64]{0,2,1:T(8,128)(2,1)} %bitcast.235, pred[320,1600]{1,0:T(8,128)(4,1)} %broadcast_compare_fusion, bf16[1600,2,64]{0,2,1:T(8,128)(2,1)} %bitcast.247, bf16[320,2,64]{0,2,1:T(8,128)(2,1)} %bitcast.275, f32[320,2]{0,1:T(2,128)} %bitcast.315), kind=kOutput, calls=%fused_computation.126 | convolution fusion | flops 267307200 | bytes 1579520 | tf_op jit(solution)/shard_map/hqk,khd->qhd/dot_general | solution.py:55
  131.6 4.3 %fusion.240 = f32[2,320]{1,0:T(2,128)} fusion(pred[320,1600]{1,0:T(8,128)(4,1)} %broadcast_compare_fusion, bf16[1600,2,64]{0,2,1:T(8,128)(2,1)} %bitcast.248, bf16[320,2,64]{0,2,1:T(8,128)(2,1)} %bitcast.272), kind=kOutput, calls=%fused_computation.310 | convolution fusion | flops 136193600 | bytes 1006080 | tf_op jit(solution)/shard_map/sub | solution.py:51
  135.9 4.4 %fusion.94 = f32[320,2,64]{0,2,1:T(8,128)} fusion(bf16[1600,2,64]{0,2,1:T(8,128)(2,1)} %bitcast.236, pred[320,1600]{1,0:T(8,128)(4,1)} %broadcast_compare_fusion, bf16[1600,2,64]{0,2,1:T(8,128)(2,1)} %bitcast.249, bf16[320,2,64]{0,2,1:T(8,128)(2,1)} %bitcast.273, f32[320,2]{0,1:T(2,128)} %bitcast.316), kind=kOutput, calls=%fused_computation.128 | convolution fusion | flops 267307200 | bytes 1579520 | tf_op jit(solution)/shard_map/hqk,khd->qhd/dot_general | solution.py:55
  144.9 3.7 %fusion.241 = f32[2,320]{1,0:T(2,128)S(1)} fusion(pred[320,1600]{1,0:T(8,128)(4,1)} %broadcast_compare_fusion, bf16[1600,2,64]{0,2,1:T(8,128)(2,1)} %bitcast.250, bf16[320,2,64]{0,2,1:T(8,128)(2,1)} %bitcast.270), kind=kOutput, calls=%fused_computation.311 | convolution fusion | flops 136193600 | bytes 1006080 | tf_op jit(solution)/shard_map/sub | solution.py:51
  148.6 4.6 %fusion.100 = f32[320,2,64]{0,2,1:T(8,128)} fusion(bf16[1600,2,64]{0,2,1:T(8,128)(2,1)} %bitcast.237, pred[320,1600]{1,0:T(8,128)(4,1)} %broadcast_compare_fusion, bf16[1600,2,64]{0,2,1:T(8,128)(2,1)} %bitcast.251, bf16[320,2,64]{0,2,1:T(8,128)(2,1)} %bitcast.271, f32[320,2]{0,1:T(2,128)S(1)} %bitcast.317), kind=kOutput, calls=%fused_computation.130 | convolution fusion | flops 267307200 | bytes 1579520 | tf_op jit(solution)/shard_map/hqk,khd->qhd/dot_general | solution.py:55
  156.9 3.7 %fusion.242 = f32[2,320]{1,0:T(2,128)S(1)} fusion(pred[320,1600]{1,0:T(8,128)(4,1)} %broadcast_compare_fusion, bf16[1600,2,64]{0,2,1:T(8,128)(2,1)} %bitcast.252, bf16[320,2,64]{0,2,1:T(8,128)(2,1)} %bitcast.268), kind=kOutput, calls=%fused_computation.312 | convolution fusion | flops 136193600 | bytes 1006080 | tf_op jit(solution)/shard_map/sub | solution.py:51
  160.5 3.6 %fusion.106 = f32[320,2,64]{0,2,1:T(8,128)S(1)} fusion(bf16[1600,2,64]{0,2,1:T(8,128)(2,1)S(1)} %bitcast.238, pred[320,1600]{1,0:T(8,128)(4,1)} %broadcast_compare_fusion, bf16[1600,2,64]{0,2,1:T(8,128)(2,1)} %bitcast.253, bf16[320,2,64]{0,2,1:T(8,128)(2,1)} %bitcast.269, f32[320,2]{0,1:T(2,128)S(1)} %bitcast.318), kind=kOutput, calls=%fused_computation.132 | convolution fusion | flops 267307200 | bytes 1579520 | tf_op jit(solution)/shard_map/hqk,khd->qhd/dot_general | solution.py:55
  166.2 3.7 %fusion.243 = f32[2,320]{1,0:T(2,128)S(1)} fusion(pred[320,1600]{1,0:T(8,128)(4,1)} %broadcast_compare_fusion, bf16[1600,2,64]{0,2,1:T(8,128)(2,1)} %bitcast.254, bf16[320,2,64]{0,2,1:T(8,128)(2,1)S(1)} %bitcast.266), kind=kOutput, calls=%fused_computation.313 | convolution fusion | flops 136193600 | bytes 1006080 | tf_op jit(solution)/shard_map/sub | solution.py:51
  175.3 3.5 %fusion.244 = f32[2,320]{1,0:T(2,128)S(1)} fusion(pred[320,1600]{1,0:T(8,128)(4,1)S(1)} %copy-done.9, bf16[1600,2,64]{0,2,1:T(8,128)(2,1)} %bitcast.240, bf16[320,2,64]{0,2,1:T(8,128)(2,1)} %bitcast.264), kind=kOutput, calls=%fused_computation.314 | convolution fusion | flops 136193600 | bytes 1006080 | tf_op jit(solution)/shard_map/sub | solution.py:51
  178.8 3.3 %fusion.118 = f32[320,2,64]{0,2,1:T(8,128)S(1)} fusion(bf16[1600,2,64]{0,2,1:T(8,128)(2,1)} %bitcast.233, pred[320,1600]{1,0:T(8,128)(4,1)S(1)} %copy-done.9, bf16[1600,2,64]{0,2,1:T(8,128)(2,1)} %bitcast.241, bf16[320,2,64]{0,2,1:T(8,128)(2,1)} %bitcast.265, f32[320,2]{0,1:T(2,128)S(1)} %bitcast.312), kind=kOutput, calls=%fused_computation.136 | convolution fusion | flops 267307200 | bytes 1579520 | tf_op jit(solution)/shard_map/hqk,khd->qhd/dot_general | solution.py:55
  183.9 5.6 %collective-permute-start.9 = (bf16[15,1024]{1,0:T(8,128)(2,1)S(1)}, bf16[15,1024]{1,0:T(8,128)(2,1)S(1)}, u32[]{:S(2)}, u32[]{:S(2)}) collective-permute-start(bf16[15,1024]{1,0:T(8,128)(2,1)S(1)} %get-tuple-element.24), channel_id=1, source_target_pairs={{2,0},{4,2},{6,4},{8,6},{10,8},{12,10},{14,12},{16,14},{18,16},{20... | collective-permute-start | bytes 92168 | tf_op jit(solution)/shard_map/ppermute | solution.py:23
  191.5 5.6 %collective-permute-done.8 = bf16[15,1024]{1,0:T(8,128)(2,1)S(1)} collective-permute-done((bf16[15,1024]{1,0:T(8,128)(2,1)S(1)}, bf16[15,1024]{1,0:T(8,128)(2,1)S(1)}, u32[]{:S(2)}, u32[]{:S(2)}) %collective-permute-start.8) | collective-permute-done | bytes 30752 | tf_op jit(solution)/shard_map/ppermute | solution.py:22
  197.5 15.6 %fusion.229 = (f32[320]{0:T(512)S(1)}, f32[320,1024]{1,0:T(8,128)S(1)}) fusion(f32[1024]{0:T(1024)S(1)} %bitcast.290, bf16[15,1024]{1,0:T(8,128)(2,1)S(1)} %collective-permute-done.9, bf16[320,1024]{1,0:T(8,128)(2,1)S(1)} %add_convert_fusion, pred[320]{0:T(512)(128)(4,1)S(1)} %get-tuple-element.93, f32[1024]{0:T(1024)S(1)} %bitcast.291, ...), kind=kLoop, calls=%fused_computation.300 | loop fusion | flops 69795520 | bytes 2165376 | tf_op jit(solution)/shard_map/reduce_sum | solution.py:100
  (195 shorter events, 79.4 us)
Async XLA Ops:
  0.0 38.9 %collective-permute-start = (bf16[320,1024]{1,0:T(8,128)(2,1)}, bf16[320,1024]{1,0:T(8,128)(2,1)}, u32[]{:S(2)}, u32[]{:S(2)}) collective-permute-start(bf16[320,1024]{1,0:T(8,128)(2,1)} %param.10), channel_id=1, source_target_pairs={{0,4},{2,6},{4,8},{6,10},{8,12},{10,14},{12,16},{14,18},{16,20},{1... | collective-permute-start | bytes 1966088 | tf_op jit(solution)/shard_map/ppermute | solution.py:12
  3.4 48.1 %collective-permute-start.1 = (bf16[320,1024]{1,0:T(8,128)(2,1)}, bf16[320,1024]{1,0:T(8,128)(2,1)S(1)}, u32[]{:S(2)}, u32[]{:S(2)}) collective-permute-start(bf16[320,1024]{1,0:T(8,128)(2,1)} %param.10), channel_id=1, source_target_pairs={{0,2},{2,4},{4,6},{6,8},{8,10},{10,12},{12,14},{14,16},{16,18},{18... | collective-permute-start | bytes 1966088 | tf_op jit(solution)/shard_map/ppermute | solution.py:12
  6.8 48.5 %collective-permute-start.2 = (bf16[320,1024]{1,0:T(8,128)(2,1)}, bf16[320,1024]{1,0:T(8,128)(2,1)S(1)}, u32[]{:S(2)}, u32[]{:S(2)}) collective-permute-start(bf16[320,1024]{1,0:T(8,128)(2,1)} %param.10), channel_id=1, source_target_pairs={{2,0},{4,2},{6,4},{8,6},{10,8},{12,10},{14,12},{16,14},{18,16},{20... | collective-permute-start | bytes 1966088 | tf_op jit(solution)/shard_map/ppermute | solution.py:12
  11.1 64.7 %collective-permute-start.3 = (bf16[320,1024]{1,0:T(8,128)(2,1)}, bf16[320,1024]{1,0:T(8,128)(2,1)S(1)}, u32[]{:S(2)}, u32[]{:S(2)}) collective-permute-start(bf16[320,1024]{1,0:T(8,128)(2,1)} %param.10), channel_id=1, source_target_pairs={{4,0},{6,2},{8,4},{10,6},{12,8},{14,10},{16,12},{18,14},{20,16},{2... | collective-permute-start | bytes 1966088 | tf_op jit(solution)/shard_map/ppermute | solution.py:12
  13.5 64.8 %collective-permute-start.4 = (bf16[320,1024]{1,0:T(8,128)(2,1)}, bf16[320,1024]{1,0:T(8,128)(2,1)S(1)}, u32[]{:S(2)}, u32[]{:S(2)}) collective-permute-start(bf16[320,1024]{1,0:T(8,128)(2,1)} %param.9), channel_id=1, source_target_pairs={{0,4},{2,6},{4,8},{6,10},{8,12},{10,14},{12,16},{14,18},{16,20},{1... | collective-permute-start | bytes 1966088 | tf_op jit(solution)/shard_map/ppermute | solution.py:12
  24.4 14.5 %copy-start.4 = (bf16[320,1024]{1,0:T(8,128)(2,1)S(1)}, bf16[320,1024]{1,0:T(8,128)(2,1)}, u32[]{:S(2)}) copy-start(bf16[320,1024]{1,0:T(8,128)(2,1)} %param.9) | copy-start | bytes 1966084
  38.9 16.4 %copy-start.3 = (bf16[320,1024]{1,0:T(8,128)(2,1)S(1)}, bf16[320,1024]{1,0:T(8,128)(2,1)}, u32[]{:S(2)}) copy-start(bf16[320,1024]{1,0:T(8,128)(2,1)} %param.10) | copy-start | bytes 1966084
  38.9 39.4 %collective-permute-start.5 = (bf16[320,1024]{1,0:T(8,128)(2,1)S(1)}, bf16[320,1024]{1,0:T(8,128)(2,1)}, u32[]{:S(2)}, u32[]{:S(2)}) collective-permute-start(bf16[320,1024]{1,0:T(8,128)(2,1)S(1)} %copy-done.4), channel_id=1, source_target_pairs={{0,2},{2,4},{4,6},{6,8},{8,10},{10,12},{12,14},{14,16},{16,18},{18... | collective-permute-start | bytes 1966088 | tf_op jit(solution)/shard_map/ppermute | solution.py:12
  51.5 28.0 %collective-permute-start.6 = (bf16[320,1024]{1,0:T(8,128)(2,1)S(1)}, bf16[320,1024]{1,0:T(8,128)(2,1)}, u32[]{:S(2)}, u32[]{:S(2)}) collective-permute-start(bf16[320,1024]{1,0:T(8,128)(2,1)S(1)} %copy-done.4), channel_id=1, source_target_pairs={{2,0},{4,2},{6,4},{8,6},{10,8},{12,10},{14,12},{16,14},{18,16},{20... | collective-permute-start | bytes 1966088 | tf_op jit(solution)/shard_map/ppermute | solution.py:12
  55.4 34.4 %collective-permute-start.7 = (bf16[320,1024]{1,0:T(8,128)(2,1)S(1)}, bf16[320,1024]{1,0:T(8,128)(2,1)}, u32[]{:S(2)}, u32[]{:S(2)}) collective-permute-start(bf16[320,1024]{1,0:T(8,128)(2,1)S(1)} %copy-done.4), channel_id=1, source_target_pairs={{4,0},{6,2},{8,4},{10,6},{12,8},{14,10},{16,12},{18,14},{20,16},{2... | collective-permute-start | bytes 1966088 | tf_op jit(solution)/shard_map/ppermute | solution.py:12
  183.3 13.8 %copy-start.17 = (f32[1,1024]{1,0:T(1,128)S(1)}, f32[1,1024]{1,0:T(1,128)}, u32[]{:S(2)}) copy-start(f32[1,1024]{1,0:T(1,128)} %get-tuple-element.61) | copy-start | bytes 12292
  183.3 13.8 %copy-start.18 = (f32[1,1024]{1,0:T(1,128)S(1)}, f32[1,1024]{1,0:T(1,128)}, u32[]{:S(2)}) copy-start(f32[1,1024]{1,0:T(1,128)} %get-tuple-element.62) | copy-start | bytes 12292
  183.4 13.8 %copy-start.19 = (f32[1,1024]{1,0:T(1,128)S(1)}, f32[1,1024]{1,0:T(1,128)}, u32[]{:S(2)}) copy-start(f32[1,1024]{1,0:T(1,128)} %get-tuple-element.63) | copy-start | bytes 12292
  183.4 13.8 %copy-start.20 = (f32[1,1024]{1,0:T(1,128)S(1)}, f32[1,1024]{1,0:T(1,128)}, u32[]{:S(2)}) copy-start(f32[1,1024]{1,0:T(1,128)} %get-tuple-element.33) | copy-start | bytes 12292
  183.4 13.8 %copy-start.21 = (f32[1,1024]{1,0:T(1,128)S(1)}, f32[1,1024]{1,0:T(1,128)}, u32[]{:S(2)}) copy-start(f32[1,1024]{1,0:T(1,128)} %get-tuple-element.34) | copy-start | bytes 12292
  183.4 13.8 %copy-start.22 = (f32[1,1024]{1,0:T(1,128)S(1)}, f32[1,1024]{1,0:T(1,128)}, u32[]{:S(2)}) copy-start(f32[1,1024]{1,0:T(1,128)} %get-tuple-element.35) | copy-start | bytes 12292
  183.4 13.8 %copy-start.23 = (f32[1,1024]{1,0:T(1,128)S(1)}, f32[1,1024]{1,0:T(1,128)}, u32[]{:S(2)}) copy-start(f32[1,1024]{1,0:T(1,128)} %get-tuple-element.36) | copy-start | bytes 12292
  183.4 13.8 %copy-start.24 = (f32[1,1024]{1,0:T(1,128)S(1)}, f32[1,1024]{1,0:T(1,128)}, u32[]{:S(2)}) copy-start(f32[1,1024]{1,0:T(1,128)} %get-tuple-element.37) | copy-start | bytes 12292
  183.4 13.8 %copy-start.25 = (f32[1,1024]{1,0:T(1,128)S(1)}, f32[1,1024]{1,0:T(1,128)}, u32[]{:S(2)}) copy-start(f32[1,1024]{1,0:T(1,128)} %get-tuple-element.38) | copy-start | bytes 12292
  183.4 13.8 %copy-start.26 = (f32[1,1024]{1,0:T(1,128)S(1)}, f32[1,1024]{1,0:T(1,128)}, u32[]{:S(2)}) copy-start(f32[1,1024]{1,0:T(1,128)} %get-tuple-element.39) | copy-start | bytes 12292
  183.9 7.6 %collective-permute-start.9 = (bf16[15,1024]{1,0:T(8,128)(2,1)S(1)}, bf16[15,1024]{1,0:T(8,128)(2,1)S(1)}, u32[]{:S(2)}, u32[]{:S(2)}) collective-permute-start(bf16[15,1024]{1,0:T(8,128)(2,1)S(1)} %get-tuple-element.24), channel_id=1, source_target_pairs={{2,0},{4,2},{6,4},{8,6},{10,8},{12,10},{14,12},{16,14},{18,16},{20... | collective-permute-start | bytes 92168 | tf_op jit(solution)/shard_map/ppermute | solution.py:23
  189.5 7.6 %collective-permute-start.8 = (bf16[15,1024]{1,0:T(8,128)(2,1)S(1)}, bf16[15,1024]{1,0:T(8,128)(2,1)S(1)}, u32[]{:S(2)}, u32[]{:S(2)}) collective-permute-start(bf16[15,1024]{1,0:T(8,128)(2,1)S(1)} %get-tuple-element.23), channel_id=1, source_target_pairs={{0,2},{2,4},{4,6},{6,8},{8,10},{10,12},{12,14},{14,16},{16,18},{18... | collective-permute-start | bytes 92168 | tf_op jit(solution)/shard_map/ppermute | solution.py:22
  197.5 16.0 %copy-start.39 = (f32[1024]{0:T(1024)S(1)}, f32[1024]{0:T(1024)}, u32[]{:S(2)}) copy-start(f32[1024]{0:T(1024)} %param.15) | copy-start | bytes 12292
  197.5 16.0 %copy-start.40 = (f32[1024]{0:T(1024)S(1)}, f32[1024]{0:T(1024)}, u32[]{:S(2)}) copy-start(f32[1024]{0:T(1024)} %param.14) | copy-start | bytes 12292
  (38 other events, 401.4 us)
where the time goes:
time: 220 us; the launch traced here: 215 us
  matrix products  61.2 us (28%)
  local copies, waits for them, and re-layouts  55.3 us (25%)
  starting transfers between devices  42.6 us (19%)
  waiting for transfers between devices  32.1 us (15%)
  other arithmetic  22.7 us (10%)
    ppermute x8, starting transfers between devices, passed_along(): return lax.ppermute(array, axis, pairs)  35 us
    dot_general x8, matrix products, attend(): jnp.einsum('hqk,khd->qhd', weights, value_group, preferred_element_type=j...  31.1 us
    sub x8, matrix products, attend(): probs = jnp.where(same_utt, jnp.exp(scores - row_max), jnp.float32(0.0))  30.1 us
    ppermute x8, waiting for transfers between devices, passed_along(): return lax.ppermute(array, axis, pairs)  26.5 us
    reduce_sum x1, other arithmetic, local(): mean_val = jnp.mean(conv_sum, axis=1, keepdims=True)  15.6 us
    slice x9, local copies, waits for them, and re-layouts, attend(): key_rows[:, first_col:first_col + group_width].reshape(-1, 2, HD)  13.5 us
    slice x9, local copies, waits for them, and re-layouts, attend(): query_rows[:, first_col:first_col + group_width].reshape(-1, 2, HD)  12.4 us
    slice x9, local copies, waits for them, and re-layouts, attend(): value_rows[:, first_col:first_col + group_width].reshape(-1, 2, HD)  12.3 us
  transfers between devices with their start and end apart: 10, of which 3 were waited for; matrix products, arithmetic and copies ran while one was open for 13% of the time, Pallas kernels for 0%

commit v1 on v0

v1 whole, which is shorter than its diff:
```python
import functools

import jax
import jax.numpy as jnp
from jax import lax
from jax.experimental import pallas as pl
from jax.experimental.pallas import tpu as pltpu
from jax.sharding import PartitionSpec as P

HD = 64
LANES = 128
GROUP = 4
EDGE = 16
SAME = 2048.0
MIB = 1 << 20

ANY = pl.BlockSpec(memory_space=pl.ANY)
VMEM = pl.BlockSpec(memory_space=pltpu.VMEM)
SMEM = pl.BlockSpec(memory_space=pltpu.SMEM)


def utterance_of(positions, ends):
    return jnp.sum((ends[None, :] <= positions[:, None]).astype(jnp.int32), axis=1)


def split_kernel(cols, which, *refs):
    n_in = len(refs) - GROUP - 1
    srcs, outs, sem = refs[:n_in], refs[n_in:-1], refs[-1]
    copies = []
    for m in range(GROUP):
        first = pl.multiple_of(which[m] * cols, LANES)
        for i, src in enumerate(srcs):
            copies.append(
                pltpu.make_async_copy(
                    src.at[:, pl.ds(first, cols)],
                    outs[m].at[:, pl.ds(i * cols, cols)],
                    sem.at[m * n_in + i],
                )
            )
    for copy in copies:
        copy.start()
    for copy in copies:
        copy.wait()


def split_columns(which, *arrays):
    rows, width = arrays[0].shape
    cols = width // GROUP
    shape = jax.ShapeDtypeStruct((rows, cols * len(arrays)), arrays[0].dtype)
    return pl.pallas_call(
        functools.partial(split_kernel, cols),
        out_shape=[shape] * GROUP,
        in_specs=[SMEM] + [ANY] * len(arrays),
        out_specs=[ANY] * GROUP,
        scratch_shapes=[pltpu.SemaphoreType.DMA((GROUP * len(arrays),))],
        name="split_columns",
    )(which, *arrays)


def attend_kernel(rows, q_rows, widths, meta, place, starts, ends, *refs):
    q_in, kv_in, outs = refs[:GROUP], refs[GROUP : 3 * GROUP], refs[3 * GROUP : 4 * GROUP]
    q_buf, kv_buf, oh_buf, ctx_buf, q_sem, kv_sem, out_sem = refs[4 * GROUP :]
    heads_cols = q_buf.shape[2]
    copies = []
    for i, src in enumerate(kv_in):
        at = pl.multiple_of(place[i] * rows, 16)
        copies.append(pltpu.make_async_copy(src, kv_buf.at[pl.ds(at, rows), :], kv_sem.at[i]))
    for m, src in enumerate(q_in):
        copies.append(pltpu.make_async_copy(src, q_buf.at[m], q_sem.at[m]))
    for copy in copies:
        copy.start()

    def one_hot(first, n, value):
        frame = first + lax.broadcasted_iota(jnp.int32, (n, starts.shape[1]), 0)
        inside = (frame >= starts[...]) & (frame < ends[...])
        return jnp.where(inside, jnp.float32(value), jnp.float32(0.0)).astype(jnp.bfloat16)

    step = rows // 2

    @pl.loop(0, kv_buf.shape[0] // step)
    def _(i):
        at = pl.multiple_of(i * step, 16)
        oh_buf[pl.ds(at, step), :] = one_hot(meta[0] + at, step, 1.0)

    for copy in copies:
        copy.wait()

    blocks = q_buf.shape[1] // q_rows
    lane = lax.broadcasted_iota(jnp.int32, (1, LANES), 1)
    scale = HD**-0.5
    halves = [
        jnp.where(lane // HD == h, jnp.float32(scale), jnp.float32(0.0)).astype(jnp.bfloat16)
        for h in range(2)
    ]

    def block(m, b, width):
        t = m * blocks + b
        low = pl.multiple_of(meta[1 + GROUP + t], 16)
        first = pl.multiple_of(b * q_rows, 16)
        oh_q = one_hot(meta[1 + m] + first, q_rows, SAME)
        oh_k = oh_buf[pl.ds(low, width), :]
        ones = jnp.ones((width, LANES), jnp.bfloat16)
        for pair in range(heads_cols // LANES):
            cols = slice(pair * LANES, (pair + 1) * LANES)
            v_cols = slice(heads_cols + pair * LANES, heads_cols + (pair + 1) * LANES)
            q = q_buf[m, pl.ds(first, q_rows), cols]
            k = jnp.concatenate([kv_buf[pl.ds(low, width), cols], oh_k], axis=1)
            v = jnp.concatenate([kv_buf[pl.ds(low, width), v_cols], ones], axis=1)
            got = []
            for h in range(2):
                q_h = jnp.concatenate([q * halves[h], oh_q], axis=1)
                s = lax.dot_general(
                    q_h, k, (((1,), (1,)), ((), ())), preferred_element_type=jnp.float32
                )
                p = jnp.exp(s - jnp.max(s, axis=1, keepdims=True)).astype(jnp.bfloat16)
                o = jnp.dot(p, v, preferred_element_type=jnp.float32)
                got.append(o[:, :LANES] / o[:, LANES:])
            ctx = jnp.where(lane < HD, got[0], got[1]).astype(jnp.bfloat16)
            ctx_buf[m, pl.ds(first, q_rows), cols] = ctx

    @pl.loop(0, GROUP * blocks)
    def _(t):
        m, b = t // blocks, t % blocks
        need = meta[1 + GROUP + GROUP * blocks + t]
        below = 0
        for width in widths:

            @pl.when((need > below) & (need <= width))
            def _(width=width):
                block(m, b, width)

            below = width

    copies = [
        pltpu.make_async_copy(ctx_buf.at[m], outs[m], out_sem.at[m]) for m in range(GROUP)
    ]
    for copy in copies:
        copy.start()
    for copy in copies:
        copy.wait()


def attend(rows, q_rows, widths, meta, place, starts, ends, q_parts, kv_parts):
    ext, cols = q_parts[0].shape
    keys = 2 * GROUP * rows
    shape = jax.ShapeDtypeStruct((ext, cols), jnp.bfloat16)
    dma = pltpu.SemaphoreType.DMA
    return pl.pallas_call(
        functools.partial(attend_kernel, rows, q_rows, widths),
        out_shape=[shape] * GROUP,
        in_specs=[SMEM, SMEM, VMEM, VMEM] + [ANY] * (3 * GROUP),
        out_specs=[ANY] * GROUP,
        scratch_shapes=[
            pltpu.VMEM((GROUP, ext, cols), jnp.bfloat16),
            pltpu.VMEM((keys, 2 * cols), jnp.bfloat16),
            pltpu.VMEM((keys, starts.shape[1]), jnp.bfloat16),
            pltpu.VMEM((GROUP, ext, cols), jnp.bfloat16),
            dma((GROUP,)),
            dma((2 * GROUP,)),
            dma((GROUP,)),
        ],
        compiler_params=pltpu.CompilerParams(vmem_limit_bytes=40 * MIB),
        name="attend",
    )(meta, place, starts, ends, *q_parts, *kv_parts)


def finish_kernel(block_rows, taps, meta, starts, ends, *refs):
    ctx_in = refs[:GROUP]
    res, res_before, res_after, kernel, gain, shift, out = refs[GROUP : GROUP + 7]
    mixed, window, conv = refs[GROUP + 7 :]
    rows, width = res.shape
    tiles = width // LANES
    per = tiles // GROUP
    half = taps // 2
    n_blocks = rows // block_rows
    for m in range(GROUP):
        for t in range(per):
            cols = slice(t * LANES, (t + 1) * LANES)
            mixed[meta[1 + m] * per + t] = ctx_in[m][:, cols].astype(jnp.float32)
    for t in range(tiles):
        cols = slice(t * LANES, (t + 1) * LANES)
        for first, part in ((0, res_before), (EDGE, res), (EDGE + rows, res_after)):
            at = slice(first, first + part.shape[0])
            total = part[:, cols].astype(jnp.float32) + mixed[t, at, :]
            mixed[t, at, :] = total.astype(jnp.bfloat16).astype(jnp.float32)

    span = block_rows + 2 * EDGE

    @pl.loop(0, n_blocks)
    def _(b):
        top = pl.multiple_of(b * block_rows, 8)
        first_frame = meta[0] + top
        around = first_frame - EDGE + lax.broadcasted_iota(jnp.int32, (span, LANES), 0)
        frame = first_frame + lax.broadcasted_iota(jnp.int32, (block_rows, LANES), 0)

        @pl.loop(meta[1 + GROUP + b], meta[1 + GROUP + n_blocks + b] + 1)
        def _(u):
            low, high = starts[u], ends[u]
            kept = (around >= low) & (around < high)
            mine = (frame >= low) & (frame < high)
            for t in range(tiles):
                window[t] = jnp.where(kept, mixed[t, pl.ds(top, span), :], jnp.float32(0.0))
            for t in range(tiles):
                cols = slice(t * LANES, (t + 1) * LANES)
                total = jnp.zeros((block_rows, LANES), jnp.float32)
                for tap in range(taps):
                    at = tap + EDGE - half
                    total = total + window[t, at : at + block_rows, :] * kernel[tap : tap + 1, cols]
                conv[t] = jnp.where(mine, total, conv[t])

        values = [conv[t] for t in range(tiles)]
        mean = jnp.sum(sum(values), axis=1, keepdims=True) / width
        centred = [x - mean for x in values]
        var = jnp.sum(sum([x * x for x in centred]), axis=1, keepdims=True) / width
        inverse = 1.0 / jnp.sqrt(var + 1e-05)
        for t in range(tiles):
            cols = slice(t * LANES, (t + 1) * LANES)
            normed = centred[t] * inverse * gain[:, cols] + shift[:, cols]
            gated = normed * jax.nn.sigmoid(normed)
            own = mixed[t, pl.ds(pl.multiple_of(top + EDGE, 8), block_rows), :]
            out[pl.ds(pl.multiple_of(top, 16), block_rows), cols] = (own + gated).astype(
                jnp.bfloat16
            )


def finish(block_rows, meta, starts, ends, ctx_parts, res, before, after, kernel, gain, shift):
    rows, width = res.shape
    tiles = width // LANES
    return pl.pallas_call(
        functools.partial(finish_kernel, block_rows, kernel.shape[0]),
        out_shape=jax.ShapeDtypeStruct((rows, width), jnp.bfloat16),
        in_specs=[SMEM, SMEM, SMEM] + [VMEM] * (GROUP + 6),
        out_specs=VMEM,
        scratch_shapes=[
            pltpu.VMEM((tiles, rows + 2 * EDGE, LANES), jnp.float32),
            pltpu.VMEM((tiles, block_rows + 2 * EDGE, LANES), jnp.float32),
            pltpu.VMEM((tiles, block_rows, LANES), jnp.float32),
        ],
        compiler_params=pltpu.CompilerParams(vmem_limit_bytes=40 * MIB),
        name="finish",
    )(meta, starts, ends, *ctx_parts, res, before, after, kernel, gain, shift)


def local(query, key, value, residual, lengths, depth_kernel, gain, shift):
    rows, width = query.shape
    peers = lax.axis_size("seq")
    frames = rows * peers
    me = lax.axis_index("seq")
    member = me % GROUP
    others = jnp.arange(GROUP, dtype=jnp.int32) ^ member
    halo = 2 * rows
    base = (me - member) * rows
    key_base = base - halo
    keys = GROUP * rows + 2 * halo

    def swap(array, m):
        return lax.ppermute(array, "seq", [(i, i ^ m) for i in range(peers)])

    def move(array, by):
        pairs = [(i, i + by(i)) for i in range(peers)]
        return lax.ppermute(array, "seq", [(i, j) for i, j in pairs if 0 <= j < peers])

    near = lambda i: -GROUP if i % GROUP < GROUP // 2 else GROUP
    far = lambda i: -near(i)

    kv = split_columns(others, key, value)
    kv_group = [kv[0]] + [swap(kv[m], m) for m in range(1, GROUP)]
    kv_halo = [move(kv_group[m], near if m < 2 else far) for m in range(GROUP)]

    last = jnp.concatenate([query[rows - EDGE :], residual[rows - EDGE :]], axis=1)
    initial = jnp.concatenate([query[:EDGE], residual[:EDGE]], axis=1)
    before = move(last, lambda i: 1)
    after = move(initial, lambda i: -1)
    query_ext = jnp.concatenate([before[:, :width], query, after[:, :width]], axis=0)
    q_out = split_columns(others, query_ext)
    q_group = [q_out[0]] + [swap(q_out[m], m) for m in range(1, GROUP)]

    ends = jnp.cumsum(lengths).astype(jnp.int32)
    starts = ends - lengths
    n_utts = lengths.shape[0]
    q_rows = (rows + 2 * EDGE) // 2
    halves = jnp.arange(2, dtype=jnp.int32)
    block_first = base + others[:, None] * rows
    first_own = jnp.where(halves == 0, 0, q_rows - EDGE)
    last_own = jnp.where(halves == 0, q_rows - EDGE - 1, rows - 1)
    first_utt = utterance_of((block_first + first_own).reshape(-1), ends)
    last_utt = utterance_of((block_first + last_own).reshape(-1), ends)
    low = (jnp.maximum(starts[first_utt] - key_base, 0) // 16) * 16
    high = jnp.minimum(ends[last_utt] - key_base, keys)
    need = high - low
    most = -(-(q_rows + 2 * halo + 16) // LANES) * LANES
    widths = sorted({min(w, most) for w in (256, 512, 768, 1024, most)})
    taken = functools.reduce(
        lambda later, w: jnp.where(need <= w, w, later), widths[::-1], jnp.full_like(need, most)
    )
    low = jnp.minimum(low, keys - taken)
    meta = jnp.concatenate(
        [key_base[None], base + others * rows - EDGE, low, need]
    ).astype(jnp.int32)
    at_group = others + GROUP // 2
    at_halo = jnp.where(others < GROUP // 2, others + 3 * GROUP // 2, others - GROUP // 2)
    place = jnp.concatenate([at_group, at_halo]).astype(jnp.int32)
    pad = -n_utts % LANES
    lane_starts = jnp.pad(starts, (0, pad))[None, :]
    lane_ends = jnp.pad(ends, (0, pad))[None, :]
    ctx = attend(
        rows, q_rows, widths, meta, place, lane_starts, lane_ends, q_group, kv_group + kv_halo
    )
    ctx_group = [ctx[0]] + [swap(ctx[m], m) for m in range(1, GROUP)]

    block_rows = 32
    n_blocks = rows // block_rows
    block_tops = me * rows + jnp.arange(n_blocks, dtype=jnp.int32) * block_rows
    meta_out = jnp.concatenate(
        [
            (me * rows)[None],
            others,
            utterance_of(block_tops, ends),
            utterance_of(block_tops + block_rows - 1, ends),
        ]
    ).astype(jnp.int32)
    return finish(
        block_rows,
        meta_out,
        starts,
        ends,
        ctx_group,
        residual,
        before[:, width:],
        after[:, width:],
        depth_kernel,
        gain[None, :],
        shift[None, :],
    )


def solution(mesh):
    return jax.shard_map(
        local,
        mesh=mesh,
        in_specs=(
            P(("dp", "seq"), None),
            P(("dp", "seq"), None),
            P(("dp", "seq"), None),
            P(("dp", "seq"), None),
            P("dp"),
            P(),
            P(),
            P(),
        ),
        out_specs=P(("dp", "seq"), None),
        check_vma=False,
    )
```

time: 220 us -> 146 us (0.66)
  the two profiles are of different devices: /device:TPU:16 before, /device:TPU:0 now
where the time goes in v1:
time: 146 us; the launch traced here: 145 us
  Pallas kernels  89.6 us (61%)
  starting transfers between devices  34.8 us (24%)
  waiting for transfers between devices  14.8 us (10%)
  local copies, waits for them, and re-layouts  3.33 us (2%)
  other arithmetic  2.45 us (2%)
    pallas_call x2, Pallas kernels, split_columns(): pl.pallas_call(functools.partial(split_kernel, cols), out_shape=[shape] *...  65.3 us
    ppermute x6, starting transfers between devices, move(): lax.ppermute(array, 'seq', [(i, j) for i, j in pairs if 0 <= j < peers])  18.5 us
    pallas_call x1, Pallas kernels, attend(): pl.pallas_call(functools.partial(attend_kernel, rows, q_rows, widths), ou...  17 us
    ppermute x9, starting transfers between devices, swap(): return lax.ppermute(array, 'seq', [(i, i ^ m) for i in range(peers)])  16.4 us
    ppermute x9, waiting for transfers between devices, swap(): return lax.ppermute(array, 'seq', [(i, i ^ m) for i in range(peers)])  14.1 us
    pallas_call x1, Pallas kernels, finish(): pl.pallas_call(functools.partial(finish_kernel, block_rows, kernel.shape[...  7.26 us
  transfers between devices with their start and end apart: 15, of which 5 were waited for; matrix products, arithmetic and copies ran while one was open for 3% of the time, Pallas kernels for 45%

profile of v1, /device:TPU:0, one launch (start us, length us, event | category | flops | bytes accessed | tf_op | source)
XLA Modules:
  0.0 145.3 jit_solution(1833226154265460455)
XLA Ops:
  0.0 0.8 fusion.5
  0.8 1.3 collective-permute-start.1
  2.2 5.5 %collective-permute-start = (bf16[16,2048]{1,0:T(8,128)(2,1)S(1)}, bf16[16,2048]{1,0:T(8,128)(2,1)S(1)}, u32[]{:S(2)}, u32[]{:S(2)}) collective-permute-start(bf16[16,2048]{1,0:T(8,128)(2,1)S(1)} %pad_maximum_fusion.1), channel_id=1, source_target_pairs={{0,2},{2,4},{4,6},{6,8},{8,10},{10,12},{12,14},{14,16},{16,18},{18... | collective-permute-start | bytes 196616 | tf_op jit(solution)/shard_map/ppermute | solution.py:261
  8.3 41.5 %split_columns.3 = (bf16[320,512]{1,0:T(8,128)(2,1)}, bf16[320,512]{1,0:T(8,128)(2,1)}, bf16[320,512]{1,0:T(8,128)(2,1)}, bf16[320,512]{1,0:T(8,128)(2,1)}) custom-call(s32[4]{0:T(128)} %iota_xor_fusion.which, bf16[320,1024]{1,0:T(8,128)(2,1)} %refs_0_.1, bf16[320,1024]{1,0:T(8,128)(2,1)} %refs_1_.1), custom_call_target="tpu_custom_call" | custom-call | tf_op jit(solution)/shard_map/split_columns/pallas_call | solution.py:50
  49.8 3.0 %collective-permute-start.5 = (bf16[320,512]{1,0:T(8,128)(2,1)}, bf16[320,512]{1,0:T(8,128)(2,1)S(1)}, u32[]{:S(2)}, u32[]{:S(2)}) collective-permute-start(bf16[320,512]{1,0:T(8,128)(2,1)} %get-tuple-element.22), channel_id=1, source_target_pairs={{0,2},{2,0},{4,6},{6,4},{8,10},{10,8},{12,14},{14,12},{16,18},{18,... | collective-permute-start | bytes 983048 | tf_op jit(solution)/shard_map/ppermute | solution.py:257
  52.8 2.4 %collective-permute-start.6 = (bf16[320,512]{1,0:T(8,128)(2,1)}, bf16[320,512]{1,0:T(8,128)(2,1)S(1)}, u32[]{:S(2)}, u32[]{:S(2)}) collective-permute-start(bf16[320,512]{1,0:T(8,128)(2,1)} %get-tuple-element.23), channel_id=1, source_target_pairs={{0,4},{2,6},{4,0},{6,2},{8,12},{10,14},{12,8},{14,10},{16,20},{18,... | collective-permute-start | bytes 983048 | tf_op jit(solution)/shard_map/ppermute | solution.py:257
  57.4 0.9 pad_maximum_fusion.refs_0_
  58.3 23.8 %split_columns.2 = (bf16[352,256]{1,0:T(8,128)(2,1)}, bf16[352,256]{1,0:T(8,128)(2,1)}, bf16[352,256]{1,0:T(8,128)(2,1)}, bf16[352,256]{1,0:T(8,128)(2,1)}) custom-call(s32[4]{0:T(128)} %iota_xor_fusion.which, bf16[352,1024]{1,0:T(8,128)(2,1)} %pad_maximum_fusion.refs_0_), custom_call_target="tpu_custom_call" | custom-call | tf_op jit(solution)/shard_map/split_columns/pallas_call | solution.py:50
  82.1 1.5 %collective-permute-start.2 = (bf16[352,256]{1,0:T(8,128)(2,1)}, bf16[352,256]{1,0:T(8,128)(2,1)S(1)}, u32[]{:S(2)}, u32[]{:S(2)}) collective-permute-start(bf16[352,256]{1,0:T(8,128)(2,1)} %get-tuple-element.18), channel_id=1, source_target_pairs={{0,2},{2,0},{4,6},{6,4},{8,10},{10,8},{12,14},{14,12},{16,18},{18,... | collective-permute-start | bytes 540680 | tf_op jit(solution)/shard_map/ppermute | solution.py:257
  83.6 2.0 %collective-permute-start.3 = (bf16[352,256]{1,0:T(8,128)(2,1)}, bf16[352,256]{1,0:T(8,128)(2,1)S(1)}, u32[]{:S(2)}, u32[]{:S(2)}) collective-permute-start(bf16[352,256]{1,0:T(8,128)(2,1)} %get-tuple-element.19), channel_id=1, source_target_pairs={{0,4},{2,6},{4,0},{6,2},{8,12},{10,14},{12,8},{14,10},{16,20},{18,... | collective-permute-start | bytes 540680 | tf_op jit(solution)/shard_map/ppermute | solution.py:257
  85.6 2.2 %collective-permute-done.2.refs_1_ = bf16[352,256]{1,0:T(8,128)(2,1)S(1)} collective-permute-done((bf16[352,256]{1,0:T(8,128)(2,1)}, bf16[352,256]{1,0:T(8,128)(2,1)S(1)}, u32[]{:S(2)}, u32[]{:S(2)}) %collective-permute-start.2) | collective-permute-done | bytes 180256 | tf_op jit(solution)/shard_map/ppermute | solution.py:257
  87.8 1.3 collective-permute-start.8
  89.1 1.3 collective-permute-start.9
  90.5 5.2 %collective-permute-start.10 = (bf16[320,512]{1,0:T(8,128)(2,1)S(1)}, bf16[320,512]{1,0:T(8,128)(2,1)S(1)}, u32[]{:S(2)}, u32[]{:S(2)}) collective-permute-start(bf16[320,512]{1,0:T(8,128)(2,1)S(1)} %collective-permute-done.6.refs_6_), channel_id=1, source_target_pairs={{0,8},{2,10},{8,16},{10,18},{12,4},{14,6},{16,24},{18,26},{20,12},... | collective-permute-start | bytes 983048 | tf_op jit(solution)/shard_map/ppermute | solution.py:261
  95.7 3.9 %collective-permute-start.11 = (bf16[320,512]{1,0:T(8,128)(2,1)S(1)}, bf16[320,512]{1,0:T(8,128)(2,1)S(1)}, u32[]{:S(2)}, u32[]{:S(2)}) collective-permute-start(bf16[320,512]{1,0:T(8,128)(2,1)S(1)} %collective-permute-done.7.refs_7_), channel_id=1, source_target_pairs={{0,8},{2,10},{8,16},{10,18},{12,4},{14,6},{16,24},{18,26},{20,12},... | collective-permute-start | bytes 983048 | tf_op jit(solution)/shard_map/ppermute | solution.py:261
  99.7 0.8 collective-permute-start.4
  100.6 5.7 %collective-permute-done.4.refs_3_ = bf16[352,256]{1,0:T(8,128)(2,1)S(1)} collective-permute-done((bf16[352,256]{1,0:T(8,128)(2,1)}, bf16[352,256]{1,0:T(8,128)(2,1)S(1)}, u32[]{:S(2)}, u32[]{:S(2)}) %collective-permute-start.4) | collective-permute-done | bytes 180256 | tf_op jit(solution)/shard_map/ppermute | solution.py:257
  107.1 0.9 copy-done.2
  108.0 17.0 %attend.1 = (bf16[352,256]{1,0:T(8,128)(2,1)S(1)}, bf16[352,256]{1,0:T(8,128)(2,1)S(1)}, bf16[352,256]{1,0:T(8,128)(2,1)S(1)}, bf16[352,256]{1,0:T(8,128)(2,1)S(1)}) custom-call(s32[21]{0:T(128)S(1)} %pad_add_fusion.1.meta, s32[8]{0:T(128)S(1)} %pad_add_fusion.2.place, s32[1,128]{1,0:T(1,128)S(1)} %get-tuple-element.56.starts, ...), custom_call_target="tpu_custom_call" | custom-call | tf_op jit(solution)/shard_map/attend/pallas_call | solution.py:148
  125.0 1.5 %collective-permute-start.12 = (bf16[352,256]{1,0:T(8,128)(2,1)S(1)}, bf16[352,256]{1,0:T(8,128)(2,1)S(1)}, u32[]{:S(2)}, u32[]{:S(2)}) collective-permute-start(bf16[352,256]{1,0:T(8,128)(2,1)S(1)} %get-tuple-element.26), channel_id=1, source_target_pairs={{0,2},{2,0},{4,6},{6,4},{8,10},{10,8},{12,14},{14,12},{16,18},{18,... | collective-permute-start | bytes 540680 | tf_op jit(solution)/shard_map/ppermute | solution.py:257
  126.5 5.1 %collective-permute-start.13 = (bf16[352,256]{1,0:T(8,128)(2,1)S(1)}, bf16[352,256]{1,0:T(8,128)(2,1)S(1)}, u32[]{:S(2)}, u32[]{:S(2)}) collective-permute-start(bf16[352,256]{1,0:T(8,128)(2,1)S(1)} %get-tuple-element.27), channel_id=1, source_target_pairs={{0,4},{2,6},{4,0},{6,2},{8,12},{10,14},{12,8},{14,10},{16,20},{18,... | collective-permute-start | bytes 540680 | tf_op jit(solution)/shard_map/ppermute | solution.py:257
  131.9 4.7 %collective-permute-done.13.refs_2_ = bf16[352,256]{1,0:T(8,128)(2,1)S(1)} collective-permute-done((bf16[352,256]{1,0:T(8,128)(2,1)S(1)}, bf16[352,256]{1,0:T(8,128)(2,1)S(1)}, u32[]{:S(2)}, u32[]{:S(2)}) %collective-permute-start.13) | collective-permute-done | bytes 180256 | tf_op jit(solution)/shard_map/ppermute | solution.py:257
  136.6 1.4 collective-permute-done.14.refs_3_
  138.0 7.3 %finish.1 = bf16[320,1024]{1,0:T(8,128)(2,1)} custom-call(s32[25]{0:T(128)S(1)} %pad_add_fusion.meta, s32[16]{0:T(128)S(1)} %sub.42.starts, s32[16]{0:T(128)S(1)} %reduce.ends, bf16[352,256]{1,0:T(8,128)(2,1)S(1)} %get-tuple-element.25.refs_0_, bf16[352,256]{1,0:T(8,128)(2,1)S(1)} %collective-permute-done.12.refs_1_, ...), custom_call_target="tpu_custom_call" | custom-call | tf_op jit(solution)/shard_map/finish/pallas_call | solution.py:229
  (59 shorter events, 3.9 us)
Async XLA Ops:
  0.8 56.5 %collective-permute-start.1 = (bf16[16,2048]{1,0:T(8,128)(2,1)S(1)}, bf16[16,2048]{1,0:T(8,128)(2,1)S(1)}, u32[]{:S(2)}, u32[]{:S(2)}) collective-permute-start(bf16[16,2048]{1,0:T(8,128)(2,1)S(1)} %pad_maximum_fusion.2), channel_id=1, source_target_pairs={{2,0},{4,2},{6,4},{8,6},{10,8},{12,10},{14,12},{16,14},{18,16},{20... | collective-permute-start | bytes 196616 | tf_op jit(solution)/shard_map/ppermute | solution.py:261
  2.1 53.3 %copy-start.8 = (s32[16]{0:T(128)S(1)}, s32[16]{0:T(128)}, u32[]{:S(2)}) copy-start(s32[16]{0:T(128)} %param.12) | copy-start | bytes 196
  2.2 55.2 %collective-permute-start = (bf16[16,2048]{1,0:T(8,128)(2,1)S(1)}, bf16[16,2048]{1,0:T(8,128)(2,1)S(1)}, u32[]{:S(2)}, u32[]{:S(2)}) collective-permute-start(bf16[16,2048]{1,0:T(8,128)(2,1)S(1)} %pad_maximum_fusion.1), channel_id=1, source_target_pairs={{0,2},{2,4},{4,6},{6,8},{8,10},{10,12},{12,14},{14,16},{16,18},{18... | collective-permute-start | bytes 196616 | tf_op jit(solution)/shard_map/ppermute | solution.py:261
  49.8 7.6 %copy-start.6 = (bf16[320,1024]{1,0:T(8,128)(2,1)S(1)}, bf16[320,1024]{1,0:T(8,128)(2,1)}, u32[]{:S(2)}) copy-start(bf16[320,1024]{1,0:T(8,128)(2,1)} %param.8) | copy-start | bytes 1966084
  49.8 39.3 %collective-permute-start.5 = (bf16[320,512]{1,0:T(8,128)(2,1)}, bf16[320,512]{1,0:T(8,128)(2,1)S(1)}, u32[]{:S(2)}, u32[]{:S(2)}) collective-permute-start(bf16[320,512]{1,0:T(8,128)(2,1)} %get-tuple-element.22), channel_id=1, source_target_pairs={{0,2},{2,0},{4,6},{6,4},{8,10},{10,8},{12,14},{14,12},{16,18},{18,... | collective-permute-start | bytes 983048 | tf_op jit(solution)/shard_map/ppermute | solution.py:257
  52.8 37.6 %collective-permute-start.6 = (bf16[320,512]{1,0:T(8,128)(2,1)}, bf16[320,512]{1,0:T(8,128)(2,1)S(1)}, u32[]{:S(2)}, u32[]{:S(2)}) collective-permute-start(bf16[320,512]{1,0:T(8,128)(2,1)} %get-tuple-element.23), channel_id=1, source_target_pairs={{0,4},{2,6},{4,0},{6,2},{8,12},{10,14},{12,8},{14,10},{16,20},{18,... | collective-permute-start | bytes 983048 | tf_op jit(solution)/shard_map/ppermute | solution.py:257
  55.2 40.4 %collective-permute-start.7 = (bf16[320,512]{1,0:T(8,128)(2,1)}, bf16[320,512]{1,0:T(8,128)(2,1)S(1)}, u32[]{:S(2)}, u32[]{:S(2)}) collective-permute-start(bf16[320,512]{1,0:T(8,128)(2,1)} %get-tuple-element.24), channel_id=1, source_target_pairs={{0,6},{2,4},{4,2},{6,0},{8,14},{10,12},{12,10},{14,8},{16,22},{18,... | collective-permute-start | bytes 983048 | tf_op jit(solution)/shard_map/ppermute | solution.py:257
  58.3 29.6 %copy-start.1 = (bf16[320,512]{1,0:T(8,128)(2,1)S(1)}, bf16[320,512]{1,0:T(8,128)(2,1)}, u32[]{:S(2)}) copy-start(bf16[320,512]{1,0:T(8,128)(2,1)} %get-tuple-element.21.refs_4_) | copy-start | bytes 983044
  82.1 5.8 %collective-permute-start.2 = (bf16[352,256]{1,0:T(8,128)(2,1)}, bf16[352,256]{1,0:T(8,128)(2,1)S(1)}, u32[]{:S(2)}, u32[]{:S(2)}) collective-permute-start(bf16[352,256]{1,0:T(8,128)(2,1)} %get-tuple-element.18), channel_id=1, source_target_pairs={{0,2},{2,0},{4,6},{6,4},{8,10},{10,8},{12,14},{14,12},{16,18},{18,... | collective-permute-start | bytes 540680 | tf_op jit(solution)/shard_map/ppermute | solution.py:257
  83.6 16.1 %collective-permute-start.3 = (bf16[352,256]{1,0:T(8,128)(2,1)}, bf16[352,256]{1,0:T(8,128)(2,1)S(1)}, u32[]{:S(2)}, u32[]{:S(2)}) collective-permute-start(bf16[352,256]{1,0:T(8,128)(2,1)} %get-tuple-element.19), channel_id=1, source_target_pairs={{0,4},{2,6},{4,0},{6,2},{8,12},{10,14},{12,8},{14,10},{16,20},{18,... | collective-permute-start | bytes 540680 | tf_op jit(solution)/shard_map/ppermute | solution.py:257
  87.8 18.5 %collective-permute-start.8 = (bf16[320,512]{1,0:T(8,128)(2,1)S(1)}, bf16[320,512]{1,0:T(8,128)(2,1)S(1)}, u32[]{:S(2)}, u32[]{:S(2)}) collective-permute-start(bf16[320,512]{1,0:T(8,128)(2,1)S(1)} %copy-done.1), channel_id=1, source_target_pairs={{4,12},{6,14},{8,0},{10,2},{12,20},{14,22},{16,8},{18,10},{20,28},... | collective-permute-start | bytes 983048 | tf_op jit(solution)/shard_map/ppermute | solution.py:261
  89.1 17.2 %collective-permute-start.9 = (bf16[320,512]{1,0:T(8,128)(2,1)S(1)}, bf16[320,512]{1,0:T(8,128)(2,1)S(1)}, u32[]{:S(2)}, u32[]{:S(2)}) collective-permute-start(bf16[320,512]{1,0:T(8,128)(2,1)S(1)} %collective-permute-done.5.refs_5_), channel_id=1, source_target_pairs={{4,12},{6,14},{8,0},{10,2},{12,20},{14,22},{16,8},{18,10},{20,28},... | collective-permute-start | bytes 983048 | tf_op jit(solution)/shard_map/ppermute | solution.py:261
  90.5 15.8 %collective-permute-start.10 = (bf16[320,512]{1,0:T(8,128)(2,1)S(1)}, bf16[320,512]{1,0:T(8,128)(2,1)S(1)}, u32[]{:S(2)}, u32[]{:S(2)}) collective-permute-start(bf16[320,512]{1,0:T(8,128)(2,1)S(1)} %collective-permute-done.6.refs_6_), channel_id=1, source_target_pairs={{0,8},{2,10},{8,16},{10,18},{12,4},{14,6},{16,24},{18,26},{20,12},... | collective-permute-start | bytes 983048 | tf_op jit(solution)/shard_map/ppermute | solution.py:261
  95.7 11.4 %collective-permute-start.11 = (bf16[320,512]{1,0:T(8,128)(2,1)S(1)}, bf16[320,512]{1,0:T(8,128)(2,1)S(1)}, u32[]{:S(2)}, u32[]{:S(2)}) collective-permute-start(bf16[320,512]{1,0:T(8,128)(2,1)S(1)} %collective-permute-done.7.refs_7_), channel_id=1, source_target_pairs={{0,8},{2,10},{8,16},{10,18},{12,4},{14,6},{16,24},{18,26},{20,12},... | collective-permute-start | bytes 983048 | tf_op jit(solution)/shard_map/ppermute | solution.py:261
  99.7 6.6 %collective-permute-start.4 = (bf16[352,256]{1,0:T(8,128)(2,1)}, bf16[352,256]{1,0:T(8,128)(2,1)S(1)}, u32[]{:S(2)}, u32[]{:S(2)}) collective-permute-start(bf16[352,256]{1,0:T(8,128)(2,1)} %get-tuple-element.20), channel_id=1, source_target_pairs={{0,6},{2,4},{4,2},{6,0},{8,14},{10,12},{12,10},{14,8},{16,22},{18,... | collective-permute-start | bytes 540680 | tf_op jit(solution)/shard_map/ppermute | solution.py:257
  107.1 0.9 copy-start.2
  108.0 23.8 %copy-start.7 = (s32[4]{0:T(128)S(1)}, s32[4]{0:T(128)}, u32[]{:S(2)}) copy-start(s32[4]{0:T(128)} %iota_xor_fusion.which) | copy-start | bytes 52
  108.0 30.0 %copy-start = (bf16[320,1024]{1,0:T(8,128)(2,1)S(1)}, bf16[320,1024]{1,0:T(8,128)(2,1)}, u32[]{:S(2)}) copy-start(bf16[320,1024]{1,0:T(8,128)(2,1)} %refs_4_.1) | copy-start | bytes 1966084
  108.0 30.0 %copy-start.3 = (f32[31,1024]{1,0:T(8,128)S(1)}, f32[31,1024]{1,0:T(8,128)}, u32[]{:S(2)}) copy-start(f32[31,1024]{1,0:T(8,128)} %refs_7_.1) | copy-start | bytes 380932
  108.0 30.0 %copy-start.4 = (f32[1024]{0:T(1024)S(1)}, f32[1024]{0:T(1024)}, u32[]{:S(2)}) copy-start(f32[1024]{0:T(1024)} %param.14) | copy-start | bytes 12292
  108.0 30.0 %copy-start.5 = (f32[1024]{0:T(1024)S(1)}, f32[1024]{0:T(1024)}, u32[]{:S(2)}) copy-start(f32[1024]{0:T(1024)} %param.15) | copy-start | bytes 12292
  125.0 6.9 %collective-permute-start.12 = (bf16[352,256]{1,0:T(8,128)(2,1)S(1)}, bf16[352,256]{1,0:T(8,128)(2,1)S(1)}, u32[]{:S(2)}, u32[]{:S(2)}) collective-permute-start(bf16[352,256]{1,0:T(8,128)(2,1)S(1)} %get-tuple-element.26), channel_id=1, source_target_pairs={{0,2},{2,0},{4,6},{6,4},{8,10},{10,8},{12,14},{14,12},{16,18},{18,... | collective-permute-start | bytes 540680 | tf_op jit(solution)/shard_map/ppermute | solution.py:257
  126.5 10.0 %collective-permute-start.13 = (bf16[352,256]{1,0:T(8,128)(2,1)S(1)}, bf16[352,256]{1,0:T(8,128)(2,1)S(1)}, u32[]{:S(2)}, u32[]{:S(2)}) collective-permute-start(bf16[352,256]{1,0:T(8,128)(2,1)S(1)} %get-tuple-element.27), channel_id=1, source_target_pairs={{0,4},{2,6},{4,0},{6,2},{8,12},{10,14},{12,8},{14,10},{16,20},{18,... | collective-permute-start | bytes 540680 | tf_op jit(solution)/shard_map/ppermute | solution.py:257
  131.6 6.4 %collective-permute-start.14 = (bf16[352,256]{1,0:T(8,128)(2,1)S(1)}, bf16[352,256]{1,0:T(8,128)(2,1)S(1)}, u32[]{:S(2)}, u32[]{:S(2)}) collective-permute-start(bf16[352,256]{1,0:T(8,128)(2,1)S(1)} %get-tuple-element.28), channel_id=1, source_target_pairs={{0,6},{2,4},{4,2},{6,0},{8,14},{10,12},{12,10},{14,8},{16,22},{18,... | collective-permute-start | bytes 540680 | tf_op jit(solution)/shard_map/ppermute | solution.py:257

commit v2 on v1

--- a/solution.py
+++ b/solution.py
@@ -24,23 +24,11 @@
 
 
 def split_kernel(cols, which, *refs):
-    n_in = len(refs) - GROUP - 1
-    srcs, outs, sem = refs[:n_in], refs[n_in:-1], refs[-1]
-    copies = []
+    srcs, outs = refs[:-GROUP], refs[-GROUP:]
     for m in range(GROUP):
         first = pl.multiple_of(which[m] * cols, LANES)
         for i, src in enumerate(srcs):
-            copies.append(
-                pltpu.make_async_copy(
-                    src.at[:, pl.ds(first, cols)],
-                    outs[m].at[:, pl.ds(i * cols, cols)],
-                    sem.at[m * n_in + i],
-                )
-            )
-    for copy in copies:
-        copy.start()
-    for copy in copies:
-        copy.wait()
+            outs[m][:, i * cols : (i + 1) * cols] = src[:, pl.ds(first, cols)]
 
 
 def split_columns(which, *arrays):
@@ -50,9 +38,9 @@
     return pl.pallas_call(
         functools.partial(split_kernel, cols),
         out_shape=[shape] * GROUP,
-        in_specs=[SMEM] + [ANY] * len(arrays),
-        out_specs=[ANY] * GROUP,
-        scratch_shapes=[pltpu.SemaphoreType.DMA((GROUP * len(arrays),))],
+        in_specs=[SMEM] + [VMEM] * len(arrays),
+        out_specs=[VMEM] * GROUP,
+        compiler_params=pltpu.CompilerParams(vmem_limit_bytes=16 * MIB),
         name="split_columns",
     )(which, *arrays)
 

time: 146 us -> 91.1 us (0.62)
  Pallas kernels: 89.6 us -> 26.9 us
  waiting for transfers between devices: 14.8 us -> 22.3 us
  other arithmetic: 2.45 us -> 0.98 us
    pallas_call x2, Pallas kernels: 65.3 us -> 1.35 us  [split_columns(): pl.pallas_call(functools.partial(split_kernel, cols), out_shape=[shape] *...]
    ppermute x9, waiting for transfers between devices: 14.1 us -> 20.2 us  [swap(): return lax.ppermute(array, 'seq', [(i, i ^ m) for i in range(peers)])]
    pallas_call x1, Pallas kernels: 17 us -> 18.6 us  [attend(): pl.pallas_call(functools.partial(attend_kernel, rows, q_rows, widths), ou...]
  transfers between devices with their start and end apart: 15 -> 15, of which waited for: 5 -> 5; matrix products, arithmetic and copies ran while one was open for 3% -> 3% of each run, Pallas kernels for 45% -> 1%
where the time goes in v2:
time: 91.1 us; the launch traced here: 91.2 us
  starting transfers between devices  36.2 us (40%)
  Pallas kernels  26.9 us (30%)
  waiting for transfers between devices  22.3 us (24%)
  local copies, waits for them, and re-layouts  4.57 us (5%)
  other arithmetic  0.98 us (1%)
    ppermute x9, waiting for transfers between devices, swap(): return lax.ppermute(array, 'seq', [(i, i ^ m) for i in range(peers)])  20.2 us
    pallas_call x1, Pallas kernels, attend(): pl.pallas_call(functools.partial(attend_kernel, rows, q_rows, widths), ou...  18.6 us
    ppermute x6, starting transfers between devices, move(): lax.ppermute(array, 'seq', [(i, j) for i, j in pairs if 0 <= j < peers])  18.5 us
    ppermute x9, starting transfers between devices, swap(): return lax.ppermute(array, 'seq', [(i, i ^ m) for i in range(peers)])  17.7 us
    pallas_call x1, Pallas kernels, finish(): pl.pallas_call(functools.partial(finish_kernel, block_rows, kernel.shape[...  6.97 us
    unnamed x16, local copies, waits for them, and re-layouts  2.2 us
    ppermute x6, waiting for transfers between devices, move(): lax.ppermute(array, 'seq', [(i, j) for i, j in pairs if 0 <= j < peers])  2.06 us
  transfers between devices with their start and end apart: 15, of which 5 were waited for; matrix products, arithmetic and copies ran while one was open for 3% of the time, Pallas kernels for 1%

profile of v2, /device:TPU:0, one launch (start us, length us, event | category | flops | bytes accessed | tf_op | source)
XLA Modules:
  0.0 91.2 jit_solution(1192304615456930088)
XLA Ops:
  0.0 0.8 fusion.5
  0.8 1.3 %collective-permute-start.1 = (bf16[16,2048]{1,0:T(8,128)(2,1)S(1)}, bf16[16,2048]{1,0:T(8,128)(2,1)S(1)}, u32[]{:S(2)}, u32[]{:S(2)}) collective-permute-start(bf16[16,2048]{1,0:T(8,128)(2,1)S(1)} %pad_maximum_fusion.2), channel_id=1, source_target_pairs={{2,0},{4,2},{6,4},{8,6},{10,8},{12,10},{14,12},{16,14},{18,16},{20... | collective-permute-start | bytes 196616 | tf_op jit(solution)/shard_map/ppermute | solution.py:249
  2.2 5.5 %collective-permute-start = (bf16[16,2048]{1,0:T(8,128)(2,1)S(1)}, bf16[16,2048]{1,0:T(8,128)(2,1)S(1)}, u32[]{:S(2)}, u32[]{:S(2)}) collective-permute-start(bf16[16,2048]{1,0:T(8,128)(2,1)S(1)} %pad_maximum_fusion.1), channel_id=1, source_target_pairs={{0,2},{2,4},{4,6},{6,8},{8,10},{10,12},{12,14},{14,16},{16,18},{18... | collective-permute-start | bytes 196616 | tf_op jit(solution)/shard_map/ppermute | solution.py:249
  7.7 1.1 %copy-done.1 = bf16[320,1024]{1,0:T(8,128)(2,1)S(1)} copy-done((bf16[320,1024]{1,0:T(8,128)(2,1)S(1)}, bf16[320,1024]{1,0:T(8,128)(2,1)}, u32[]{:S(2)}) %copy-start.1) | copy-done | bytes 655384
  8.8 1.1 %copy-done.2 = bf16[320,1024]{1,0:T(8,128)(2,1)S(1)} copy-done((bf16[320,1024]{1,0:T(8,128)(2,1)S(1)}, bf16[320,1024]{1,0:T(8,128)(2,1)}, u32[]{:S(2)}) %copy-start.2) | copy-done | bytes 655384
  9.8 0.7 split_columns.3
  10.6 3.0 %collective-permute-start.5 = (bf16[320,512]{1,0:T(8,128)(2,1)S(1)}, bf16[320,512]{1,0:T(8,128)(2,1)S(1)}, u32[]{:S(2)}, u32[]{:S(2)}) collective-permute-start(bf16[320,512]{1,0:T(8,128)(2,1)S(1)} %get-tuple-element.22), channel_id=1, source_target_pairs={{0,2},{2,0},{4,6},{6,4},{8,10},{10,8},{12,14},{14,12},{16,18},{18,... | collective-permute-start | bytes 983048 | tf_op jit(solution)/shard_map/ppermute | solution.py:245
  13.6 2.4 %collective-permute-start.6 = (bf16[320,512]{1,0:T(8,128)(2,1)S(1)}, bf16[320,512]{1,0:T(8,128)(2,1)S(1)}, u32[]{:S(2)}, u32[]{:S(2)}) collective-permute-start(bf16[320,512]{1,0:T(8,128)(2,1)S(1)} %get-tuple-element.23), channel_id=1, source_target_pairs={{0,4},{2,6},{4,0},{6,2},{8,12},{10,14},{12,8},{14,10},{16,20},{18,... | collective-permute-start | bytes 983048 | tf_op jit(solution)/shard_map/ppermute | solution.py:245
  18.8 1.5 %collective-permute-start.2 = (bf16[352,256]{1,0:T(8,128)(2,1)S(1)}, bf16[352,256]{1,0:T(8,128)(2,1)S(1)}, u32[]{:S(2)}, u32[]{:S(2)}) collective-permute-start(bf16[352,256]{1,0:T(8,128)(2,1)S(1)} %get-tuple-element.18), channel_id=1, source_target_pairs={{0,2},{2,0},{4,6},{6,4},{8,10},{10,8},{12,14},{14,12},{16,18},{18,... | collective-permute-start | bytes 540680 | tf_op jit(solution)/shard_map/ppermute | solution.py:245
  20.4 2.0 %collective-permute-start.3 = (bf16[352,256]{1,0:T(8,128)(2,1)S(1)}, bf16[352,256]{1,0:T(8,128)(2,1)S(1)}, u32[]{:S(2)}, u32[]{:S(2)}) collective-permute-start(bf16[352,256]{1,0:T(8,128)(2,1)S(1)} %get-tuple-element.19), channel_id=1, source_target_pairs={{0,4},{2,6},{4,0},{6,2},{8,12},{10,14},{12,8},{14,10},{16,20},{18,... | collective-permute-start | bytes 540680 | tf_op jit(solution)/shard_map/ppermute | solution.py:245
  22.4 9.2 %collective-permute-done.2.refs_1_ = bf16[352,256]{1,0:T(8,128)(2,1)S(1)} collective-permute-done((bf16[352,256]{1,0:T(8,128)(2,1)S(1)}, bf16[352,256]{1,0:T(8,128)(2,1)S(1)}, u32[]{:S(2)}, u32[]{:S(2)}) %collective-permute-start.2) | collective-permute-done | bytes 180256 | tf_op jit(solution)/shard_map/ppermute | solution.py:245
  31.6 1.3 %collective-permute-start.8 = (bf16[320,512]{1,0:T(8,128)(2,1)S(1)}, bf16[320,512]{1,0:T(8,128)(2,1)S(1)}, u32[]{:S(2)}, u32[]{:S(2)}) collective-permute-start(bf16[320,512]{1,0:T(8,128)(2,1)S(1)} %get-tuple-element.21.refs_4_), channel_id=1, source_target_pairs={{4,12},{6,14},{8,0},{10,2},{12,20},{14,22},{16,8},{18,10},{20,28},... | collective-permute-start | bytes 983048 | tf_op jit(solution)/shard_map/ppermute | solution.py:249
  32.9 1.3 %collective-permute-start.9 = (bf16[320,512]{1,0:T(8,128)(2,1)S(1)}, bf16[320,512]{1,0:T(8,128)(2,1)S(1)}, u32[]{:S(2)}, u32[]{:S(2)}) collective-permute-start(bf16[320,512]{1,0:T(8,128)(2,1)S(1)} %collective-permute-done.5.refs_5_), channel_id=1, source_target_pairs={{4,12},{6,14},{8,0},{10,2},{12,20},{14,22},{16,8},{18,10},{20,28},... | collective-permute-start | bytes 983048 | tf_op jit(solution)/shard_map/ppermute | solution.py:249
  34.2 5.2 %collective-permute-start.10 = (bf16[320,512]{1,0:T(8,128)(2,1)S(1)}, bf16[320,512]{1,0:T(8,128)(2,1)S(1)}, u32[]{:S(2)}, u32[]{:S(2)}) collective-permute-start(bf16[320,512]{1,0:T(8,128)(2,1)S(1)} %collective-permute-done.6.refs_6_), channel_id=1, source_target_pairs={{0,8},{2,10},{8,16},{10,18},{12,4},{14,6},{16,24},{18,26},{20,12},... | collective-permute-start | bytes 983048 | tf_op jit(solution)/shard_map/ppermute | solution.py:249
  39.5 3.9 %collective-permute-start.11 = (bf16[320,512]{1,0:T(8,128)(2,1)S(1)}, bf16[320,512]{1,0:T(8,128)(2,1)S(1)}, u32[]{:S(2)}, u32[]{:S(2)}) collective-permute-start(bf16[320,512]{1,0:T(8,128)(2,1)S(1)} %collective-permute-done.7.refs_7_), channel_id=1, source_target_pairs={{0,8},{2,10},{8,16},{10,18},{12,4},{14,6},{16,24},{18,26},{20,12},... | collective-permute-start | bytes 983048 | tf_op jit(solution)/shard_map/ppermute | solution.py:249
  43.5 1.5 %collective-permute-start.4 = (bf16[352,256]{1,0:T(8,128)(2,1)S(1)}, bf16[352,256]{1,0:T(8,128)(2,1)S(1)}, u32[]{:S(2)}, u32[]{:S(2)}) collective-permute-start(bf16[352,256]{1,0:T(8,128)(2,1)S(1)} %get-tuple-element.20), channel_id=1, source_target_pairs={{0,6},{2,4},{4,2},{6,0},{8,14},{10,12},{12,10},{14,8},{16,22},{18,... | collective-permute-start | bytes 540680 | tf_op jit(solution)/shard_map/ppermute | solution.py:245
  45.0 4.8 %collective-permute-done.4.refs_3_ = bf16[352,256]{1,0:T(8,128)(2,1)S(1)} collective-permute-done((bf16[352,256]{1,0:T(8,128)(2,1)S(1)}, bf16[352,256]{1,0:T(8,128)(2,1)S(1)}, u32[]{:S(2)}, u32[]{:S(2)}) %collective-permute-start.4) | collective-permute-done | bytes 180256 | tf_op jit(solution)/shard_map/ppermute | solution.py:245
  49.9 2.0 %collective-permute-done.11.refs_11_ = bf16[320,512]{1,0:T(8,128)(2,1)S(1)} collective-permute-done((bf16[320,512]{1,0:T(8,128)(2,1)S(1)}, bf16[320,512]{1,0:T(8,128)(2,1)S(1)}, u32[]{:S(2)}, u32[]{:S(2)}) %collective-permute-start.11) | collective-permute-done | bytes 327712 | tf_op jit(solution)/shard_map/ppermute | solution.py:249
  51.9 18.6 %attend.1 = (bf16[352,256]{1,0:T(8,128)(2,1)S(1)}, bf16[352,256]{1,0:T(8,128)(2,1)S(1)}, bf16[352,256]{1,0:T(8,128)(2,1)S(1)}, bf16[352,256]{1,0:T(8,128)(2,1)S(1)}) custom-call(s32[21]{0:T(128)S(1)} %pad_add_fusion.1.meta, s32[8]{0:T(128)S(1)} %pad_add_fusion.2.place, s32[1,128]{1,0:T(1,128)S(1)} %get-tuple-element.56.starts, ...), custom_call_target="tpu_custom_call" | custom-call | tf_op jit(solution)/shard_map/attend/pallas_call | solution.py:136
  70.5 1.5 %collective-permute-start.12 = (bf16[352,256]{1,0:T(8,128)(2,1)S(1)}, bf16[352,256]{1,0:T(8,128)(2,1)S(1)}, u32[]{:S(2)}, u32[]{:S(2)}) collective-permute-start(bf16[352,256]{1,0:T(8,128)(2,1)S(1)} %get-tuple-element.26), channel_id=1, source_target_pairs={{0,2},{2,0},{4,6},{6,4},{8,10},{10,8},{12,14},{14,12},{16,18},{18,... | collective-permute-start | bytes 540680 | tf_op jit(solution)/shard_map/ppermute | solution.py:245
  72.1 5.8 %collective-permute-start.13 = (bf16[352,256]{1,0:T(8,128)(2,1)S(1)}, bf16[352,256]{1,0:T(8,128)(2,1)S(1)}, u32[]{:S(2)}, u32[]{:S(2)}) collective-permute-start(bf16[352,256]{1,0:T(8,128)(2,1)S(1)} %get-tuple-element.27), channel_id=1, source_target_pairs={{0,4},{2,6},{4,0},{6,2},{8,12},{10,14},{12,8},{14,10},{16,20},{18,... | collective-permute-start | bytes 540680 | tf_op jit(solution)/shard_map/ppermute | solution.py:245
  78.1 4.7 %collective-permute-done.13.refs_2_ = bf16[352,256]{1,0:T(8,128)(2,1)S(1)} collective-permute-done((bf16[352,256]{1,0:T(8,128)(2,1)S(1)}, bf16[352,256]{1,0:T(8,128)(2,1)S(1)}, u32[]{:S(2)}, u32[]{:S(2)}) %collective-permute-start.13) | collective-permute-done | bytes 180256 | tf_op jit(solution)/shard_map/ppermute | solution.py:245
  82.8 1.4 %collective-permute-done.14.refs_3_ = bf16[352,256]{1,0:T(8,128)(2,1)S(1)} collective-permute-done((bf16[352,256]{1,0:T(8,128)(2,1)S(1)}, bf16[352,256]{1,0:T(8,128)(2,1)S(1)}, u32[]{:S(2)}, u32[]{:S(2)}) %collective-permute-start.14) | collective-permute-done | bytes 180256 | tf_op jit(solution)/shard_map/ppermute | solution.py:245
  84.2 7.0 %finish.1 = bf16[320,1024]{1,0:T(8,128)(2,1)} custom-call(s32[25]{0:T(128)S(1)} %pad_add_fusion.meta, s32[16]{0:T(128)S(1)} %sub.42.starts, s32[16]{0:T(128)S(1)} %reduce.ends, bf16[352,256]{1,0:T(8,128)(2,1)S(1)} %get-tuple-element.25.refs_0_, bf16[352,256]{1,0:T(8,128)(2,1)S(1)} %collective-permute-done.12.refs_1_, ...), custom_call_target="tpu_custom_call" | custom-call | tf_op jit(solution)/shard_map/finish/pallas_call | solution.py:217
  (57 shorter events, 3.3 us)
Async XLA Ops:
  0.8 17.2 %collective-permute-start.1 = (bf16[16,2048]{1,0:T(8,128)(2,1)S(1)}, bf16[16,2048]{1,0:T(8,128)(2,1)S(1)}, u32[]{:S(2)}, u32[]{:S(2)}) collective-permute-start(bf16[16,2048]{1,0:T(8,128)(2,1)S(1)} %pad_maximum_fusion.2), channel_id=1, source_target_pairs={{2,0},{4,2},{6,4},{8,6},{10,8},{12,10},{14,12},{16,14},{18,16},{20... | collective-permute-start | bytes 196616 | tf_op jit(solution)/shard_map/ppermute | solution.py:249
  2.1 14.1 %copy-start.7 = (s32[16]{0:T(128)S(1)}, s32[16]{0:T(128)}, u32[]{:S(2)}) copy-start(s32[16]{0:T(128)} %param.12) | copy-start | bytes 196
  2.2 15.9 %collective-permute-start = (bf16[16,2048]{1,0:T(8,128)(2,1)S(1)}, bf16[16,2048]{1,0:T(8,128)(2,1)S(1)}, u32[]{:S(2)}, u32[]{:S(2)}) collective-permute-start(bf16[16,2048]{1,0:T(8,128)(2,1)S(1)} %pad_maximum_fusion.1), channel_id=1, source_target_pairs={{0,2},{2,4},{4,6},{6,8},{8,10},{10,12},{12,14},{14,16},{16,18},{18... | collective-permute-start | bytes 196616 | tf_op jit(solution)/shard_map/ppermute | solution.py:249
  7.7 1.1 %copy-start.1 = (bf16[320,1024]{1,0:T(8,128)(2,1)S(1)}, bf16[320,1024]{1,0:T(8,128)(2,1)}, u32[]{:S(2)}) copy-start(bf16[320,1024]{1,0:T(8,128)(2,1)} %refs_0_.1) | copy-start | bytes 1966084
  8.8 1.1 %copy-start.2 = (bf16[320,1024]{1,0:T(8,128)(2,1)S(1)}, bf16[320,1024]{1,0:T(8,128)(2,1)}, u32[]{:S(2)}) copy-start(bf16[320,1024]{1,0:T(8,128)(2,1)} %refs_1_.1) | copy-start | bytes 1966084
  10.6 7.6 %copy-start.6 = (bf16[320,1024]{1,0:T(8,128)(2,1)S(1)}, bf16[320,1024]{1,0:T(8,128)(2,1)}, u32[]{:S(2)}) copy-start(bf16[320,1024]{1,0:T(8,128)(2,1)} %param.8) | copy-start | bytes 1966084
  10.6 22.4 %collective-permute-start.5 = (bf16[320,512]{1,0:T(8,128)(2,1)S(1)}, bf16[320,512]{1,0:T(8,128)(2,1)S(1)}, u32[]{:S(2)}, u32[]{:S(2)}) collective-permute-start(bf16[320,512]{1,0:T(8,128)(2,1)S(1)} %get-tuple-element.22), channel_id=1, source_target_pairs={{0,2},{2,0},{4,6},{6,4},{8,10},{10,8},{12,14},{14,12},{16,18},{18,... | collective-permute-start | bytes 983048 | tf_op jit(solution)/shard_map/ppermute | solution.py:245
  13.6 20.7 %collective-permute-start.6 = (bf16[320,512]{1,0:T(8,128)(2,1)S(1)}, bf16[320,512]{1,0:T(8,128)(2,1)S(1)}, u32[]{:S(2)}, u32[]{:S(2)}) collective-permute-start(bf16[320,512]{1,0:T(8,128)(2,1)S(1)} %get-tuple-element.23), channel_id=1, source_target_pairs={{0,4},{2,6},{4,0},{6,2},{8,12},{10,14},{12,8},{14,10},{16,20},{18,... | collective-permute-start | bytes 983048 | tf_op jit(solution)/shard_map/ppermute | solution.py:245
  16.0 23.5 %collective-permute-start.7 = (bf16[320,512]{1,0:T(8,128)(2,1)S(1)}, bf16[320,512]{1,0:T(8,128)(2,1)S(1)}, u32[]{:S(2)}, u32[]{:S(2)}) collective-permute-start(bf16[320,512]{1,0:T(8,128)(2,1)S(1)} %get-tuple-element.24), channel_id=1, source_target_pairs={{0,6},{2,4},{4,2},{6,0},{8,14},{10,12},{12,10},{14,8},{16,22},{18,... | collective-permute-start | bytes 983048 | tf_op jit(solution)/shard_map/ppermute | solution.py:245
  18.8 12.8 %collective-permute-start.2 = (bf16[352,256]{1,0:T(8,128)(2,1)S(1)}, bf16[352,256]{1,0:T(8,128)(2,1)S(1)}, u32[]{:S(2)}, u32[]{:S(2)}) collective-permute-start(bf16[352,256]{1,0:T(8,128)(2,1)S(1)} %get-tuple-element.18), channel_id=1, source_target_pairs={{0,2},{2,0},{4,6},{6,4},{8,10},{10,8},{12,14},{14,12},{16,18},{18,... | collective-permute-start | bytes 540680 | tf_op jit(solution)/shard_map/ppermute | solution.py:245
  20.4 23.1 %collective-permute-start.3 = (bf16[352,256]{1,0:T(8,128)(2,1)S(1)}, bf16[352,256]{1,0:T(8,128)(2,1)S(1)}, u32[]{:S(2)}, u32[]{:S(2)}) collective-permute-start(bf16[352,256]{1,0:T(8,128)(2,1)S(1)} %get-tuple-element.19), channel_id=1, source_target_pairs={{0,4},{2,6},{4,0},{6,2},{8,12},{10,14},{12,8},{14,10},{16,20},{18,... | collective-permute-start | bytes 540680 | tf_op jit(solution)/shard_map/ppermute | solution.py:245
  31.6 18.2 %collective-permute-start.8 = (bf16[320,512]{1,0:T(8,128)(2,1)S(1)}, bf16[320,512]{1,0:T(8,128)(2,1)S(1)}, u32[]{:S(2)}, u32[]{:S(2)}) collective-permute-start(bf16[320,512]{1,0:T(8,128)(2,1)S(1)} %get-tuple-element.21.refs_4_), channel_id=1, source_target_pairs={{4,12},{6,14},{8,0},{10,2},{12,20},{14,22},{16,8},{18,10},{20,28},... | collective-permute-start | bytes 983048 | tf_op jit(solution)/shard_map/ppermute | solution.py:249
  32.9 16.9 %collective-permute-start.9 = (bf16[320,512]{1,0:T(8,128)(2,1)S(1)}, bf16[320,512]{1,0:T(8,128)(2,1)S(1)}, u32[]{:S(2)}, u32[]{:S(2)}) collective-permute-start(bf16[320,512]{1,0:T(8,128)(2,1)S(1)} %collective-permute-done.5.refs_5_), channel_id=1, source_target_pairs={{4,12},{6,14},{8,0},{10,2},{12,20},{14,22},{16,8},{18,10},{20,28},... | collective-permute-start | bytes 983048 | tf_op jit(solution)/shard_map/ppermute | solution.py:249
  34.2 15.6 %collective-permute-start.10 = (bf16[320,512]{1,0:T(8,128)(2,1)S(1)}, bf16[320,512]{1,0:T(8,128)(2,1)S(1)}, u32[]{:S(2)}, u32[]{:S(2)}) collective-permute-start(bf16[320,512]{1,0:T(8,128)(2,1)S(1)} %collective-permute-done.6.refs_6_), channel_id=1, source_target_pairs={{0,8},{2,10},{8,16},{10,18},{12,4},{14,6},{16,24},{18,26},{20,12},... | collective-permute-start | bytes 983048 | tf_op jit(solution)/shard_map/ppermute | solution.py:249
  39.5 12.5 %collective-permute-start.11 = (bf16[320,512]{1,0:T(8,128)(2,1)S(1)}, bf16[320,512]{1,0:T(8,128)(2,1)S(1)}, u32[]{:S(2)}, u32[]{:S(2)}) collective-permute-start(bf16[320,512]{1,0:T(8,128)(2,1)S(1)} %collective-permute-done.7.refs_7_), channel_id=1, source_target_pairs={{0,8},{2,10},{8,16},{10,18},{12,4},{14,6},{16,24},{18,26},{20,12},... | collective-permute-start | bytes 983048 | tf_op jit(solution)/shard_map/ppermute | solution.py:249
  43.5 6.4 %collective-permute-start.4 = (bf16[352,256]{1,0:T(8,128)(2,1)S(1)}, bf16[352,256]{1,0:T(8,128)(2,1)S(1)}, u32[]{:S(2)}, u32[]{:S(2)}) collective-permute-start(bf16[352,256]{1,0:T(8,128)(2,1)S(1)} %get-tuple-element.20), channel_id=1, source_target_pairs={{0,6},{2,4},{4,2},{6,0},{8,14},{10,12},{12,10},{14,8},{16,22},{18,... | collective-permute-start | bytes 540680 | tf_op jit(solution)/shard_map/ppermute | solution.py:245
  51.9 32.3 %copy-start = (bf16[320,1024]{1,0:T(8,128)(2,1)S(1)}, bf16[320,1024]{1,0:T(8,128)(2,1)}, u32[]{:S(2)}) copy-start(bf16[320,1024]{1,0:T(8,128)(2,1)} %refs_4_.1) | copy-start | bytes 1966084
  51.9 32.3 %copy-start.3 = (f32[31,1024]{1,0:T(8,128)S(1)}, f32[31,1024]{1,0:T(8,128)}, u32[]{:S(2)}) copy-start(f32[31,1024]{1,0:T(8,128)} %refs_7_.1) | copy-start | bytes 380932
  51.9 32.3 %copy-start.4 = (f32[1024]{0:T(1024)S(1)}, f32[1024]{0:T(1024)}, u32[]{:S(2)}) copy-start(f32[1024]{0:T(1024)} %param.14) | copy-start | bytes 12292
  51.9 32.3 %copy-start.5 = (f32[1024]{0:T(1024)S(1)}, f32[1024]{0:T(1024)}, u32[]{:S(2)}) copy-start(f32[1024]{0:T(1024)} %param.15) | copy-start | bytes 12292
  70.5 7.6 %collective-permute-start.12 = (bf16[352,256]{1,0:T(8,128)(2,1)S(1)}, bf16[352,256]{1,0:T(8,128)(2,1)S(1)}, u32[]{:S(2)}, u32[]{:S(2)}) collective-permute-start(bf16[352,256]{1,0:T(8,128)(2,1)S(1)} %get-tuple-element.26), channel_id=1, source_target_pairs={{0,2},{2,0},{4,6},{6,4},{8,10},{10,8},{12,14},{14,12},{16,18},{18,... | collective-permute-start | bytes 540680 | tf_op jit(solution)/shard_map/ppermute | solution.py:245
  72.1 10.7 %collective-permute-start.13 = (bf16[352,256]{1,0:T(8,128)(2,1)S(1)}, bf16[352,256]{1,0:T(8,128)(2,1)S(1)}, u32[]{:S(2)}, u32[]{:S(2)}) collective-permute-start(bf16[352,256]{1,0:T(8,128)(2,1)S(1)} %get-tuple-element.27), channel_id=1, source_target_pairs={{0,4},{2,6},{4,0},{6,2},{8,12},{10,14},{12,8},{14,10},{16,20},{18,... | collective-permute-start | bytes 540680 | tf_op jit(solution)/shard_map/ppermute | solution.py:245
  77.8 6.4 %collective-permute-start.14 = (bf16[352,256]{1,0:T(8,128)(2,1)S(1)}, bf16[352,256]{1,0:T(8,128)(2,1)S(1)}, u32[]{:S(2)}, u32[]{:S(2)}) collective-permute-start(bf16[352,256]{1,0:T(8,128)(2,1)S(1)} %get-tuple-element.28), channel_id=1, source_target_pairs={{0,6},{2,4},{4,2},{6,0},{8,14},{10,12},{12,10},{14,8},{16,22},{18,... | collective-permute-start | bytes 540680 | tf_op jit(solution)/shard_map/ppermute | solution.py:245
